TPU v7x, 512 devices: a whole 4x8x8 slice. The times are simulated.
512 devices in a mesh: tok: 32 (over y, z_lo), col: 16 (over x, z_hi, core).
Axes of the slice: x: 4, y: 8, z: 8 (z_hi: 2, z_lo: 4; z = z_hi * 4 + z_lo), core: 2. Of those that a mesh axis runs over, the one named last changes fastest.
Arguments:
- grads: bfloat16 [2048, 27648], P('tok', 'col'), may hold values from -6 to 6
- acts: bfloat16 [2048, 5120], P('col', 'tok'), may hold values from -6 to 6
- grad_basis: bfloat16 [27648, 13824], P('col', 'tok'), may hold values from -0.0625 to 0.0625
- act_basis: bfloat16 [5120, 5120], P('tok', 'col'), may hold values from -0.15625 to 0.15625
Outputs:
- corrected_diag: float32 [13824, 5120], P('tok', 'col')
All inputs are finite; a program needn't handle non-finite values.
Results may differ from a plain program's by a relative error of at most 0.0027.
Values may be sent and summed in bfloat16 or wider, within the bound.
No kernel may reach another device: no remote copies, remote signals or barrier semaphores. Data moves between devices by JAX's collectives and lax.ppermute only.
A program may use at most 64 MiB of HBM per device.

v0:
```python
import jax
import jax.numpy as jnp
from jax import lax
from jax.sharding import PartitionSpec as P


def on_device(grads, acts, grad_basis, act_basis):
    partial_grad = jnp.dot(
        lax.all_gather(grads, "tok", axis=0, tiled=True),
        grad_basis,
        preferred_element_type=jnp.float32,
    )
    rot_grad = lax.psum(partial_grad, "col")
    sq_grad = (rot_grad * rot_grad).astype(jnp.bfloat16)
    acts_all = lax.all_gather(acts, "col", axis=0, tiled=True)
    act_share = lax.psum_scatter(
        jnp.dot(acts_all, act_basis, preferred_element_type=jnp.float32),
        "tok",
        scatter_dimension=0,
        tiled=True,
    )
    sq_act_share = (act_share * act_share).astype(jnp.bfloat16)
    sq_act = lax.all_gather(sq_act_share, "tok", axis=0, tiled=True)
    total = lax.dot_general(
        sq_grad, sq_act, (((0,), (0,)), ((), ())), preferred_element_type=jnp.float32
    )
    return total / jnp.float32(sq_grad.shape[0])


def solution(mesh):
    return jax.shard_map(
        on_device,
        mesh=mesh,
        in_specs=(P("tok", "col"), P("col", "tok"), P("col", "tok"), P("tok", "col")),
        out_specs=P("tok", "col"),
        check_vma=False,
    )
```

profile of v0, /device:TPU:48, one launch (start us, length us, event | category | flops | bytes accessed | tf_op | source)
XLA Modules:
  0.0 799.2 jit_solution(16572341921136854129)
XLA Ops:
  6.5 0.0 copy-start
  6.5 0.0 reduce-scatter.2.cloned.1.call-start
  6.5 41.8 %all_gather.10 = bf16[2048,160]{0,1:T(8,128)(2,1)S(1)} all-gather(bf16[128,160]{0,1:T(8,128)(2,1)} %param.5), channel_id=1, replica_groups=mesh['tok'=32,'col'=16] {'col'}, dimensions={0}, use_global_device_ids=true | all-gather | bytes 696320 | tf_op jit(solution)/shard_map/all_gather | solution.py:15
  48.3 3.4 fusion.3
  51.7 0.0 reduce-scatter.2.cloned.1.call-update
  51.7 0.0 all-gather.3.cloned.1.call-start
  51.8 0.7 all-gather.3.cloned.1.call-update
  52.5 0.0 all-gather.5.cloned.1.call-start
  52.5 150.4 %reduce-scatter.2.cloned.1.call-done = f32[64,320]{1,0:T(8,128)} async-done(((f32[2048,320]{1,0:T(8,128)}), f32[64,320]{1,0:T(8,128)}) %reduce-scatter.2.cloned.1.call-update) | async-done | bytes 81936 | tf_op jit(solution)/shard_map/reduce_scatter | solution.py:16
  203.0 1.5 multiply_convert_fusion.4
  204.5 0.0 all-gather.5.cloned.1.call-update
  204.5 0.0 all-reduce.2.cloned.1.call-start
  204.5 184.7 %all-gather.3.cloned.1.call-done = bf16[2048,1728]{1,0:T(8,128)(2,1)} async-done(((bf16[64,1728]{1,0:T(8,128)(2,1)}), bf16[2048,1728]{1,0:T(8,128)(2,1)}) %all-gather.3.cloned.1.call-update) | async-done | bytes 7077904 | tf_op jit(solution)/shard_map/all_gather | solution.py:9
  389.3 0.0 copy-done
  389.3 8.7 %fusion.2 = f32[2048,432]{1,0:T(8,128)} fusion(bf16[2048,1728]{1,0:T(8,128)(2,1)} %all-gather.3.cloned.1.call-done, bf16[1728,432]{0,1:T(8,128)(2,1)S(1)} %copy-done), kind=kOutput, calls=%fused_computation.4 | convolution fusion | flops 3057647616 | bytes 12109824 | tf_op jit(solution)/shard_map/dot_general | solution.py:8
  398.0 0.0 all-reduce.2.cloned.1.call-update
  398.0 138.9 %all-gather.5.cloned.1.call-done = bf16[2048,320]{1,0:T(8,128)(2,1)} async-done(((bf16[64,320]{1,0:T(8,128)(2,1)}), bf16[2048,320]{1,0:T(8,128)(2,1)}) %all-gather.5.cloned.1.call-update) | async-done | bytes 1310736 | tf_op jit(solution)/shard_map/all_gather | solution.py:23
  537.0 251.3 %all-reduce.2.cloned.1.call-done = f32[2048,432]{1,0:T(8,128)} async-done(((f32[2048,432]{1,0:T(8,128)}), f32[2048,432]{1,0:T(8,128)}) %all-reduce.2.cloned.1.call-update) | async-done | bytes 3538960 | tf_op jit(solution)/shard_map/psum | solution.py:13
  788.2 4.4 fusion.1
Async XLA Ops:
  6.5 382.7 %copy-start = (bf16[1728,432]{0,1:T(8,128)(2,1)S(1)}, bf16[1728,432]{0,1:T(8,128)(2,1)}, u32[]{:S(2)}) copy-start(bf16[1728,432]{0,1:T(8,128)(2,1)} %param.6) | copy-start | bytes 4478980
  6.5 196.4 %reduce-scatter.2.cloned.1.call-start = ((), (), s32[]{:S(2)}) async-start(), calls=%async_computation.3 | async-start | bytes 3244032 | tf_op jit(solution)/shard_map/reduce_scatter | solution.py:16
  51.7 337.6 %all-gather.3.cloned.1.call-start = ((), (), s32[]{:S(2)}) async-start(), calls=%async_computation.1 | async-start | bytes 7569408 | tf_op jit(solution)/shard_map/all_gather | solution.py:9
  52.5 484.5 %all-gather.5.cloned.1.call-start = ((), (), s32[]{:S(2)}) async-start(), calls=%async_computation.4 | async-start | bytes 1622016 | tf_op jit(solution)/shard_map/all_gather | solution.py:23
  204.5 583.7 %all-reduce.2.cloned.1.call-start = ((), (), s32[]{:S(2)}) async-start(), calls=%async_computation.2 | async-start | bytes 8388608 | tf_op jit(solution)/shard_map/psum | solution.py:13
Sparse Core Ops, SparseCore 0:
  51.8 151.0 reduce-scatter.1
  205.2 183.9 all-gather.2
  391.6 145.3 all-gather.4
  540.0 248.1 all-reduce.1
where the time goes:
time: 799 us
  waiting for transfers between devices  726 us (91%)
  blocking collectives  41.8 us (5%)
  matrix products  16.5 us (2%)
  between operations  13.1 us (2%)
    psum x1, waiting for transfers between devices, on_device(): rot_grad = lax.psum(partial_grad, 'col')  251 us
    all_gather x1, waiting for transfers between devices, on_device(): lax.all_gather(grads, 'tok', axis=0, tiled=True)  185 us
    reduce_scatter x1, waiting for transfers between devices, on_device(): lax.psum_scatter(jnp.dot(acts_all, act_basis, preferred_element_type=jnp....  150 us
    all_gather x1, waiting for transfers between devices, on_device(): sq_act = lax.all_gather(sq_act_share, 'tok', axis=0, tiled=True)  139 us
    all_gather x1, blocking collectives, on_device(): acts_all = lax.all_gather(acts, 'col', axis=0, tiled=True)  41.8 us
  transfers between devices with their start and end apart: 4, of which 4 were waited for; matrix products, arithmetic and copies ran while one was open for 1% of the time, Pallas kernels for 0%

commit v1 on v0

v1 whole, which is shorter than its diff:
```python
import jax
import jax.numpy as jnp
from jax import lax
from jax.sharding import Mesh, PartitionSpec as P

F32, BF16 = jnp.float32, jnp.bfloat16
SPLIT = (8, 4, 4, 2, 2)
AXES = ("y", "zl", "x", "zh", "core")
TOK, COL = ("y", "zl"), ("x", "zh", "core")


def dot(a, b):
    return jnp.dot(a, b, preferred_element_type=F32)


def shift(value, axis, by):
    n = lax.axis_size(axis)
    return lax.ppermute(value, axis, [(i, (i + by) % n) for i in range(n)])


def swap(value, axis, bit):
    return lax.ppermute(value, axis, [(i, i ^ bit) for i in range(lax.axis_size(axis))])


def ordered(first, mine, other):
    return jnp.stack([jnp.where(first, mine, other), jnp.where(first, other, mine)])


def squared_acts(acts, act_basis):
    rows, feats = acts.shape
    basis = lax.all_gather(act_basis, "zl", axis=0)
    part = lax.all_to_all(acts.reshape(4, rows // 4, feats), "zl", 0, 0)
    core, zh = lax.axis_index("core"), lax.axis_index("zh")
    part = ordered(zh == 0, part, swap(part, "zh", 1))
    part = lax.all_gather(part, "x", axis=0)
    part = ordered(core == 0, part, swap(part, "core", 1))
    part = part.reshape(16, 4, rows // 4, feats)
    rot = sum(dot(part[:, s].reshape(-1, feats), basis[s]) for s in range(4))
    cols = rot.shape[-1]
    rot = rot.astype(BF16).reshape(2, 8, rows // 4, cols).transpose(1, 0, 2, 3)
    rot = lax.all_to_all(rot, "y", 0, 0).astype(F32).sum(0)
    sq = lax.all_gather((rot * rot).astype(BF16), "zl", axis=0)
    sq = sq.transpose(1, 0, 2, 3).reshape(-1, cols)
    return lax.all_gather(sq, "y", axis=0, tiled=True)


def squared_grads(blocks, own_basis, other_basis):
    rows = jnp.concatenate(blocks, 0)
    part = jnp.stack([dot(rows, b).astype(BF16).reshape(8, rows.shape[0] // 8, -1) for b in (own_basis, other_basis)], 1)
    part = lax.all_to_all(part, ("core", "x"), 0, 0).astype(F32).sum(0)
    rot = part + swap(part.astype(BF16), "zh", 1).astype(F32)
    sq = (rot * rot).astype(BF16)
    sq = ordered(lax.axis_index("zl") % 2 == 0, sq[0], swap(sq[1], "zl", 1))
    sq = lax.all_gather(sq, "x", axis=0)
    sq = ordered(lax.axis_index("core") == 0, sq, swap(sq, "core", 1))
    return sq.reshape(-1, sq.shape[-1])


def on_device(grads, acts, grad_basis, act_basis):
    half = grads.shape[0]
    block = ordered(lax.axis_index("zl") < 2, grads, swap(grads, "zl", 2)).reshape(2 * half, -1)
    other_basis = swap(grad_basis, "zl", 1)
    right, left = [block], [block]
    for _ in range(3):
        right.append(shift(right[-1], "y", 1))
        left.append(shift(left[-1], "y", -1))
    last = jnp.concatenate([shift(right[3][:half], "y", 1), shift(left[3][half:], "y", -1)], 0)
    sq_act = squared_acts(acts, act_basis)
    near = squared_grads([right[1], block, left[1], left[2]], grad_basis, other_basis)
    far = squared_grads([left[3], last, right[3], right[2]], grad_basis, other_basis)
    tokens = sq_act.shape[0]
    at = (lax.axis_index("y") + 7) % 8 * (tokens // 8)
    sq_act = lax.dynamic_slice_in_dim(jnp.concatenate([sq_act, sq_act], 0), at, tokens, 0)
    total = sum(
        lax.dot_general(g, a, (((0,), (0,)), ((), ())), preferred_element_type=F32)
        for g, a in ((near, sq_act[: tokens // 2]), (far, sq_act[tokens // 2 :]))
    )
    return total / F32(tokens)


def solution(mesh):
    return jax.shard_map(
        on_device,
        mesh=Mesh(mesh.devices.reshape(SPLIT), AXES),
        in_specs=(P(TOK, COL), P(COL, TOK), P(COL, TOK), P(TOK, COL)),
        out_specs=P(TOK, COL),
        check_vma=False,
    )
```

time: 799 us -> 270 us (0.34)
  the two profiles are of different devices: /device:TPU:48 before, /device:TPU:25 now
where the time goes in v1:
time: 270 us; the launch traced here: 269 us
  starting transfers between devices  112 us (41%)
  blocking collectives  85.6 us (32%)
  waiting for transfers between devices  31.7 us (12%)
  between operations  14.1 us (5%)
  matrix products  13.4 us (5%)
  local copies, waits for them, and re-layouts  7.86 us (3%)
  other arithmetic  4.21 us (2%)
    ppermute x10, starting transfers between devices, swap(): lax.ppermute(value, axis, [(i, i ^ bit) for i in range(lax.axis_size(axis...  59.5 us
    all_gather x1, blocking collectives, squared_acts(): basis = lax.all_gather(act_basis, 'zl', axis=0)  43.3 us
    ppermute x8, starting transfers between devices, shift(): return lax.ppermute(value, axis, [(i, (i + by) % n) for i in range(n)])  25.2 us
    ppermute x8, waiting for transfers between devices, shift(): return lax.ppermute(value, axis, [(i, (i + by) % n) for i in range(n)])  24.2 us
    all_gather x2, blocking collectives, squared_grads(): sq = lax.all_gather(sq, 'x', axis=0)  20.9 us
    all_to_all x2, starting transfers between devices, squared_grads(): part = lax.all_to_all(part, ('core', 'x'), 0, 0).astype(F32).sum(0)  13.3 us
    dot_general x8, matrix products, dot(): return jnp.dot(a, b, preferred_element_type=F32)  11.5 us
    all_gather x1, blocking collectives, squared_acts(): sq = lax.all_gather((rot * rot).astype(BF16), 'zl', axis=0)  11.2 us
  transfers between devices with their start and end apart: 23, of which 7 were waited for; matrix products, arithmetic and copies ran while one was open for 7% of the time, Pallas kernels for 0%

profile of v1, /device:TPU:25, one launch (start us, length us, event | category | flops | bytes accessed | tf_op | source)
XLA Modules:
  0.0 268.7 jit_solution(7956651300268251783)
XLA Ops:
  6.5 1.6 copy.23
  8.1 7.0 %all-to-all-start.1 = ((bf16[4,32,160]{2,1,0:T(8,128)(2,1)}), bf16[4,32,160]{2,1,0:T(8,128)(2,1)S(1)}, u32[]{:S(2)}, u32[]{:S(2)}) async-start(bf16[4,32,160]{2,1,0:T(8,128)(2,1)} %bitcast.13), calls=%async_computation.1 | async-start | bytes 131072 | tf_op jit(solution)/shard_map/all_to_all | solution.py:32
  15.1 4.3 %collective-permute-start = (bf16[64,1728]{1,0:T(8,128)(2,1)}, bf16[64,1728]{1,0:T(8,128)(2,1)S(1)}, u32[]{:S(2)}, u32[]{:S(2)}) collective-permute-start(bf16[64,1728]{1,0:T(8,128)(2,1)} %param.4), channel_id=1, source_target_pairs={{0,32},{16,48},{32,0},{48,16},{1,33},{17,49},{33,1},{49,17},{2,34}... | collective-permute-start | bytes 663560 | tf_op jit(solution)/shard_map/ppermute | solution.py:22
  19.3 3.1 %collective-permute-start.4 = (bf16[1728,432]{0,1:T(8,128)(2,1)}, bf16[1728,432]{0,1:T(8,128)(2,1)}, u32[]{:S(2)}, u32[]{:S(2)}) collective-permute-start(bf16[1728,432]{0,1:T(8,128)(2,1)} %param.6), channel_id=1, source_target_pairs={{0,16},{16,0},{32,48},{48,32},{1,17},{17,1},{33,49},{49,33},{2,18}... | collective-permute-start | bytes 4478984 | tf_op jit(solution)/shard_map/ppermute | solution.py:22
  22.5 7.9 %collective-permute-start.8 = (bf16[4,32,160]{2,1,0:T(8,128)(2,1)S(1)}, bf16[4,32,160]{2,1,0:T(8,128)(2,1)S(1)}, u32[]{:S(2)}, u32[]{:S(2)}) collective-permute-start(bf16[4,32,160]{2,1,0:T(8,128)(2,1)S(1)} %all-to-all-done.1), channel_id=1, source_target_pairs={{0,2},{2,0},{1,3},{3,1},{4,6},{6,4},{5,7},{7,5},{8,10},{10,8},{9,1... | collective-permute-start | bytes 122888 | tf_op jit(solution)/shard_map/ppermute | solution.py:22
  30.4 43.3 %all-gather.2 = bf16[640,320]{1,0:T(8,128)(2,1)S(1)} all-gather(bf16[160,320]{1,0:T(8,128)(2,1)} %param.7), channel_id=4, replica_groups=mesh['y'=8,'zl'=4,'x'=4,'zh'=2,'core'=2] {'zl'}, dimensions={0}, use_global_device_ids=true | all-gather | bytes 512000 | tf_op jit(solution)/shard_map/all_gather | solution.py:31
  73.7 10.2 %all-gather.1 = bf16[8,4,32,160]{3,2,1,0:T(8,128)(2,1)S(1)} all-gather(bf16[2,4,32,160]{3,2,1,0:T(8,128)(2,1)S(1)} %pad_maximum_fusion.10), channel_id=3, replica_groups=mesh['y'=8,'zl'=4,'x'=4,'zh'=2,'core'=2] {'x'}, dimensions={0}, use_global_device_ids=true | all-gather | bytes 409600 | tf_op jit(solution)/shard_map/all_gather | solution.py:35
  84.0 8.5 %collective-permute-start.9 = (bf16[4,2,4,32,160]{4,3,2,1,0:T(8,128)(2,1)S(1)}, bf16[4,2,4,32,160]{4,3,2,1,0:T(8,128)(2,1)S(1)}, u32[]{:S(2)}, u32[]{:S(2)}) collective-permute-start(bf16[4,2,4,32,160]{4,3,2,1,0:T(8,128)(2,1)S(1)} %bitcast.85), channel_id=1, source_target_pairs={{0,1},{1,0},{2,3},{3,2},{4,5},{5,4},{6,7},{7,6},{8,9},{9,8},{10,11... | collective-permute-start | bytes 983048 | tf_op jit(solution)/shard_map/ppermute | solution.py:22
  92.6 2.1 collective-permute-start.2
  96.1 0.3 fusion.2
  96.6 0.8 copy.26
  97.4 6.9 %all-to-all-start.2 = ((bf16[8,2,32,320]{3,2,1,0:T(8,128)(2,1)}), bf16[8,2,32,320]{3,2,1,0:T(8,128)(2,1)S(1)}, u32[]{:S(2)}, u32[]{:S(2)}) async-start(bf16[8,2,32,320]{3,2,1,0:T(8,128)(2,1)} %copy.26), calls=%async_computation.2 | async-start | bytes 786432 | tf_op jit(solution)/shard_map/all_to_all | solution.py:41
  104.3 4.3 %collective-permute-start.1 = (bf16[128,1728]{1,0:T(8,128)(2,1)S(1)}, bf16[128,1728]{1,0:T(8,128)(2,1)}, u32[]{:S(2)}, u32[]{:S(2)}) collective-permute-start(bf16[128,1728]{1,0:T(8,128)(2,1)S(1)} %bitcast.100), channel_id=1, source_target_pairs={{0,64},{64,128},{128,192},{192,256},{256,320},{320,384},{384,448},... | collective-permute-start | bytes 1327112 | tf_op jit(solution)/shard_map/ppermute | solution.py:18
  108.6 1.9 collective-permute-start.3
  110.6 13.1 %collective-permute-done.1 = bf16[128,1728]{1,0:T(8,128)(2,1)} collective-permute-done((bf16[128,1728]{1,0:T(8,128)(2,1)S(1)}, bf16[128,1728]{1,0:T(8,128)(2,1)}, u32[]{:S(2)}, u32[]{:S(2)}) %collective-permute-start.1) | collective-permute-done | bytes 442400 | tf_op jit(solution)/shard_map/ppermute | solution.py:18
  123.7 4.5 %collective-permute-start.11 = (bf16[128,1728]{1,0:T(8,128)(2,1)}, bf16[128,1728]{1,0:T(8,128)(2,1)S(1)}, u32[]{:S(2)}, u32[]{:S(2)}) collective-permute-start(bf16[128,1728]{1,0:T(8,128)(2,1)} %collective-permute-done.1), channel_id=1, source_target_pairs={{0,64},{64,128},{128,192},{192,256},{256,320},{320,384},{384,448},... | collective-permute-start | bytes 1327112 | tf_op jit(solution)/shard_map/ppermute | solution.py:18
  128.3 2.2 convolution_convert_fusion.3
  130.7 1.9 collective-permute-start.10
  132.6 4.8 %collective-permute-done.11 = bf16[128,1728]{1,0:T(8,128)(2,1)S(1)} collective-permute-done((bf16[128,1728]{1,0:T(8,128)(2,1)}, bf16[128,1728]{1,0:T(8,128)(2,1)S(1)}, u32[]{:S(2)}, u32[]{:S(2)}) %collective-permute-start.11) | collective-permute-done | bytes 442400 | tf_op jit(solution)/shard_map/ppermute | solution.py:18
  137.4 5.2 %collective-permute-start.12 = (bf16[128,1728]{1,0:T(8,128)(2,1)S(1)}, bf16[128,1728]{1,0:T(8,128)(2,1)S(1)}, u32[]{:S(2)}, u32[]{:S(2)}) collective-permute-start(bf16[128,1728]{1,0:T(8,128)(2,1)S(1)} %collective-permute-done.11), channel_id=1, source_target_pairs={{0,64},{64,128},{128,192},{192,256},{256,320},{320,384},{384,448},... | collective-permute-start | bytes 1327112 | tf_op jit(solution)/shard_map/ppermute | solution.py:18
  142.7 2.8 %convolution_convert_fusion.2 = bf16[512,432]{0,1:T(8,128)(2,1)S(1)} fusion(bf16[1728,432]{0,1:T(8,128)(2,1)} %collective-permute-done.4, bf16[128,1728]{1,0:T(8,128)(2,1)} %collective-permute-done.3, bf16[128,1728]{1,0:T(8,128)(2,1)} %copy-done.3, bf16[128,1728]{1,0:T(8,128)(2,1)S(1)} %bitcast.102, bf16[128,1728]{1,0:T(8,128)(2,1)} %collective-permute-done.1), kind=kOutput, calls=%fused_computation.8 | convolution fusion | flops 771710976 | bytes 3704832 | tf_op jit(solution)/shard_map/dot_general | solution.py:13
  145.8 1.1 copy.22
  146.9 5.8 %all-to-all-start = ((bf16[8,2,64,432]{3,2,1,0:T(8,128)(2,1)}), bf16[8,2,64,432]{3,2,1,0:T(8,128)(2,1)S(1)}, u32[]{:S(2)}, u32[]{:S(2)}) async-start(bf16[8,2,64,432]{3,2,1,0:T(8,128)(2,1)} %copy.22), calls=%async_computation | async-start | bytes 2097152 | tf_op jit(solution)/shard_map/all_to_all | solution.py:50
  152.7 3.3 %collective-permute-start.13 = (bf16[64,1728]{1,0:T(8,128)(2,1)S(1)}, bf16[64,1728]{1,0:T(8,128)(2,1)S(1)}, u32[]{:S(2)}, u32[]{:S(2)}) collective-permute-start(bf16[64,1728]{1,0:T(8,128)(2,1)S(1)} %slice.79), channel_id=1, source_target_pairs={{0,64},{64,128},{128,192},{192,256},{256,320},{320,384},{384,448},... | collective-permute-start | bytes 663560 | tf_op jit(solution)/shard_map/ppermute | solution.py:18
  156.0 2.0 collective-permute-start.14
  158.1 3.0 %collective-permute-done.13 = bf16[64,1728]{1,0:T(8,128)(2,1)S(1)} collective-permute-done((bf16[64,1728]{1,0:T(8,128)(2,1)S(1)}, bf16[64,1728]{1,0:T(8,128)(2,1)S(1)}, u32[]{:S(2)}, u32[]{:S(2)}) %collective-permute-start.13) | collective-permute-done | bytes 221216 | tf_op jit(solution)/shard_map/ppermute | solution.py:18
  161.1 3.2 %collective-permute-done.14 = bf16[64,1728]{1,0:T(8,128)(2,1)S(1)} collective-permute-done((bf16[64,1728]{1,0:T(8,128)(2,1)S(1)}, bf16[64,1728]{1,0:T(8,128)(2,1)S(1)}, u32[]{:S(2)}, u32[]{:S(2)}) %collective-permute-start.14) | collective-permute-done | bytes 221216 | tf_op jit(solution)/shard_map/ppermute | solution.py:18
  164.4 1.2 copy-done.1
  165.7 2.4 convolution_convert_fusion
  168.3 2.9 %convolution_convert_fusion.1 = bf16[512,432]{0,1:T(8,128)(2,1)S(1)} fusion(bf16[512,1728]{1,0:T(8,128)(2,1)} %copy-done.1, bf16[1728,432]{0,1:T(8,128)(2,1)} %param.6), kind=kOutput, calls=%fused_computation.7 | convolution fusion | flops 764633088 | bytes 3704832 | tf_op jit(solution)/shard_map/dot_general | solution.py:13
  171.6 1.1 copy.30
  172.6 7.5 %all-to-all-start.3 = ((bf16[8,2,64,432]{3,2,1,0:T(8,128)(2,1)}), bf16[8,2,64,432]{3,2,1,0:T(8,128)(2,1)S(1)}, u32[]{:S(2)}, u32[]{:S(2)}) async-start(bf16[8,2,64,432]{3,2,1,0:T(8,128)(2,1)} %copy.30), calls=%async_computation.3 | async-start | bytes 2097152 | tf_op jit(solution)/shard_map/all_to_all | solution.py:50
  180.4 7.5 %collective-permute-start.5 = (bf16[2,64,432]{2,1,0:T(8,128)(2,1)S(1)}, bf16[2,64,432]{2,1,0:T(8,128)(2,1)S(1)}, u32[]{:S(2)}, u32[]{:S(2)}) collective-permute-start(bf16[2,64,432]{2,1,0:T(8,128)(2,1)S(1)} %convert_element_type.58), channel_id=1, source_target_pairs={{0,2},{2,0},{1,3},{3,1},{4,6},{6,4},{5,7},{7,5},{8,10},{10,8},{9,1... | collective-permute-start | bytes 331784 | tf_op jit(solution)/shard_map/ppermute | solution.py:22
  187.9 3.7 %collective-permute-done.5 = bf16[2,64,432]{2,1,0:T(8,128)(2,1)S(1)} collective-permute-done((bf16[2,64,432]{2,1,0:T(8,128)(2,1)S(1)}, bf16[2,64,432]{2,1,0:T(8,128)(2,1)S(1)}, u32[]{:S(2)}, u32[]{:S(2)}) %collective-permute-start.5) | collective-permute-done | bytes 110624 | tf_op jit(solution)/shard_map/ppermute | solution.py:22
  191.7 4.5 %collective-permute-start.6 = (bf16[64,432]{1,0:T(8,128)(2,1)S(1)}, bf16[64,432]{1,0:T(8,128)(2,1)S(1)}, u32[]{:S(2)}, u32[]{:S(2)}) collective-permute-start(bf16[64,432]{1,0:T(8,128)(2,1)S(1)} %slice_bitcast_fusion.2), channel_id=1, source_target_pairs={{0,16},{16,0},{32,48},{48,32},{1,17},{17,1},{33,49},{49,33},{2,18}... | collective-permute-start | bytes 165896 | tf_op jit(solution)/shard_map/ppermute | solution.py:22
  196.2 11.2 %all-gather.3 = bf16[8,32,320]{2,1,0:T(8,128)(2,1)S(1)} all-gather(bf16[2,32,320]{2,1,0:T(8,128)(2,1)S(1)} %multiply_convert_fusion.2), channel_id=5, replica_groups=mesh['y'=8,'zl'=4,'x'=4,'zh'=2,'core'=2] {'zl'}, dimensions={0}, use_global_device_ids=true | all-gather | bytes 204800 | tf_op jit(solution)/shard_map/all_gather | solution.py:42
  207.4 0.7 copy.27
  208.4 7.2 %collective-permute-start.15 = (bf16[2,64,432]{2,1,0:T(8,128)(2,1)S(1)}, bf16[2,64,432]{2,1,0:T(8,128)(2,1)S(1)}, u32[]{:S(2)}, u32[]{:S(2)}) collective-permute-start(bf16[2,64,432]{2,1,0:T(8,128)(2,1)S(1)} %convert_element_type.68), channel_id=1, source_target_pairs={{0,2},{2,0},{1,3},{3,1},{4,6},{6,4},{5,7},{7,5},{8,10},{10,8},{9,1... | collective-permute-start | bytes 331784 | tf_op jit(solution)/shard_map/ppermute | solution.py:22
  215.6 2.4 collective-permute-done.15
  218.1 1.9 collective-permute-start.16
  220.0 10.2 %all-gather = bf16[8,64,432]{2,1,0:T(8,128)(2,1)S(1)} all-gather(bf16[2,64,432]{2,1,0:T(8,128)(2,1)S(1)} %pad_maximum_fusion.9), channel_id=2, replica_groups=mesh['y'=8,'zl'=4,'x'=4,'zh'=2,'core'=2] {'x'}, dimensions={0}, use_global_device_ids=true | all-gather | bytes 552960 | tf_op jit(solution)/shard_map/all_gather | solution.py:54
  230.2 10.2 %collective-permute-start.7 = (bf16[4,2,64,432]{3,2,1,0:T(8,128)(2,1)S(1)}, bf16[4,2,64,432]{3,2,1,0:T(8,128)(2,1)S(1)}, u32[]{:S(2)}, u32[]{:S(2)}) collective-permute-start(bf16[4,2,64,432]{3,2,1,0:T(8,128)(2,1)S(1)} %bitcast.81), channel_id=1, source_target_pairs={{0,1},{1,0},{2,3},{3,2},{4,5},{5,4},{6,7},{7,6},{8,9},{9,8},{10,11... | collective-permute-start | bytes 1327112 | tf_op jit(solution)/shard_map/ppermute | solution.py:22
  240.4 10.7 %all-gather.4 = bf16[8,64,432]{2,1,0:T(8,128)(2,1)S(1)} all-gather(bf16[2,64,432]{2,1,0:T(8,128)(2,1)S(1)} %pad_maximum_fusion.11), channel_id=6, replica_groups=mesh['y'=8,'zl'=4,'x'=4,'zh'=2,'core'=2] {'x'}, dimensions={0}, use_global_device_ids=true | all-gather | bytes 552960 | tf_op jit(solution)/shard_map/all_gather | solution.py:54
  251.1 4.4 %collective-permute-start.17 = (bf16[4,2,64,432]{3,2,1,0:T(8,128)(2,1)S(1)}, bf16[4,2,64,432]{3,2,1,0:T(8,128)(2,1)S(1)}, u32[]{:S(2)}, u32[]{:S(2)}) collective-permute-start(bf16[4,2,64,432]{3,2,1,0:T(8,128)(2,1)S(1)} %bitcast.83), channel_id=1, source_target_pairs={{0,1},{1,0},{2,3},{3,2},{4,5},{5,4},{6,7},{7,6},{8,9},{9,8},{10,11... | collective-permute-start | bytes 1327112 | tf_op jit(solution)/shard_map/ppermute | solution.py:22
  255.6 1.3 collective-permute-done.17
  257.3 2.6 fusion
  259.9 0.5 fusion.4
  260.5 1.4 fusion.1
  (67 shorter events, 4.0 us)
Async XLA Ops:
  6.5 86.0 %copy-start = (bf16[64,1728]{1,0:T(8,128)(2,1)S(1)}, bf16[64,1728]{1,0:T(8,128)(2,1)}, u32[]{:S(2)}) copy-start(bf16[64,1728]{1,0:T(8,128)(2,1)} %param.4) | copy-start | bytes 663556
  8.1 14.4 %all-to-all-start.1 = ((bf16[4,32,160]{2,1,0:T(8,128)(2,1)}), bf16[4,32,160]{2,1,0:T(8,128)(2,1)S(1)}, u32[]{:S(2)}, u32[]{:S(2)}) async-start(bf16[4,32,160]{2,1,0:T(8,128)(2,1)} %bitcast.13), calls=%async_computation.1 | async-start | bytes 131072 | tf_op jit(solution)/shard_map/all_to_all | solution.py:32
  15.1 77.4 %collective-permute-start = (bf16[64,1728]{1,0:T(8,128)(2,1)}, bf16[64,1728]{1,0:T(8,128)(2,1)S(1)}, u32[]{:S(2)}, u32[]{:S(2)}) collective-permute-start(bf16[64,1728]{1,0:T(8,128)(2,1)} %param.4), channel_id=1, source_target_pairs={{0,32},{16,48},{32,0},{48,16},{1,33},{17,49},{33,1},{49,17},{2,34}... | collective-permute-start | bytes 663560 | tf_op jit(solution)/shard_map/ppermute | solution.py:22
  19.3 123.3 %collective-permute-start.4 = (bf16[1728,432]{0,1:T(8,128)(2,1)}, bf16[1728,432]{0,1:T(8,128)(2,1)}, u32[]{:S(2)}, u32[]{:S(2)}) collective-permute-start(bf16[1728,432]{0,1:T(8,128)(2,1)} %param.6), channel_id=1, source_target_pairs={{0,16},{16,0},{32,48},{48,32},{1,17},{17,1},{33,49},{49,33},{2,18}... | collective-permute-start | bytes 4478984 | tf_op jit(solution)/shard_map/ppermute | solution.py:22
  22.5 51.2 %collective-permute-start.8 = (bf16[4,32,160]{2,1,0:T(8,128)(2,1)S(1)}, bf16[4,32,160]{2,1,0:T(8,128)(2,1)S(1)}, u32[]{:S(2)}, u32[]{:S(2)}) collective-permute-start(bf16[4,32,160]{2,1,0:T(8,128)(2,1)S(1)} %all-to-all-done.1), channel_id=1, source_target_pairs={{0,2},{2,0},{1,3},{3,1},{4,6},{6,4},{5,7},{7,5},{8,10},{10,8},{9,1... | collective-permute-start | bytes 122888 | tf_op jit(solution)/shard_map/ppermute | solution.py:22
  84.0 10.7 %collective-permute-start.9 = (bf16[4,2,4,32,160]{4,3,2,1,0:T(8,128)(2,1)S(1)}, bf16[4,2,4,32,160]{4,3,2,1,0:T(8,128)(2,1)S(1)}, u32[]{:S(2)}, u32[]{:S(2)}) collective-permute-start(bf16[4,2,4,32,160]{4,3,2,1,0:T(8,128)(2,1)S(1)} %bitcast.85), channel_id=1, source_target_pairs={{0,1},{1,0},{2,3},{3,2},{4,5},{5,4},{6,7},{7,6},{8,9},{9,8},{10,11... | collective-permute-start | bytes 983048 | tf_op jit(solution)/shard_map/ppermute | solution.py:22
  92.6 16.0 %collective-permute-start.2 = (bf16[128,1728]{1,0:T(8,128)(2,1)S(1)}, bf16[128,1728]{1,0:T(8,128)(2,1)S(1)}, u32[]{:S(2)}, u32[]{:S(2)}) collective-permute-start(bf16[128,1728]{1,0:T(8,128)(2,1)S(1)} %bitcast.99), channel_id=1, source_target_pairs={{0,448},{64,0},{128,64},{192,128},{256,192},{320,256},{384,320},{4... | collective-permute-start | bytes 1327112 | tf_op jit(solution)/shard_map/ppermute | solution.py:18
  96.1 32.2 %copy-start.2 = (bf16[1728,432]{0,1:T(8,128)(2,1)S(1)}, bf16[1728,432]{0,1:T(8,128)(2,1)}, u32[]{:S(2)}) copy-start(bf16[1728,432]{0,1:T(8,128)(2,1)} %param.6) | copy-start | bytes 4478980
  97.4 30.8 %all-to-all-start.2 = ((bf16[8,2,32,320]{3,2,1,0:T(8,128)(2,1)}), bf16[8,2,32,320]{3,2,1,0:T(8,128)(2,1)S(1)}, u32[]{:S(2)}, u32[]{:S(2)}) async-start(bf16[8,2,32,320]{3,2,1,0:T(8,128)(2,1)} %copy.26), calls=%async_computation.2 | async-start | bytes 786432 | tf_op jit(solution)/shard_map/all_to_all | solution.py:41
  104.3 19.4 %collective-permute-start.1 = (bf16[128,1728]{1,0:T(8,128)(2,1)S(1)}, bf16[128,1728]{1,0:T(8,128)(2,1)}, u32[]{:S(2)}, u32[]{:S(2)}) collective-permute-start(bf16[128,1728]{1,0:T(8,128)(2,1)S(1)} %bitcast.100), channel_id=1, source_target_pairs={{0,64},{64,128},{128,192},{192,256},{256,320},{320,384},{384,448},... | collective-permute-start | bytes 1327112 | tf_op jit(solution)/shard_map/ppermute | solution.py:18
  108.6 21.8 %copy-start.3 = (bf16[128,1728]{1,0:T(8,128)(2,1)}, bf16[128,1728]{1,0:T(8,128)(2,1)S(1)}, u32[]{:S(2)}) copy-start(bf16[128,1728]{1,0:T(8,128)(2,1)S(1)} %collective-permute-done.2) | copy-start | bytes 1327108
  108.6 19.7 %collective-permute-start.3 = (bf16[128,1728]{1,0:T(8,128)(2,1)S(1)}, bf16[128,1728]{1,0:T(8,128)(2,1)}, u32[]{:S(2)}, u32[]{:S(2)}) collective-permute-start(bf16[128,1728]{1,0:T(8,128)(2,1)S(1)} %collective-permute-done.2), channel_id=1, source_target_pairs={{0,448},{64,0},{128,64},{192,128},{256,192},{320,256},{384,320},{4... | collective-permute-start | bytes 1327112 | tf_op jit(solution)/shard_map/ppermute | solution.py:18
  123.7 13.7 %collective-permute-start.11 = (bf16[128,1728]{1,0:T(8,128)(2,1)}, bf16[128,1728]{1,0:T(8,128)(2,1)S(1)}, u32[]{:S(2)}, u32[]{:S(2)}) collective-permute-start(bf16[128,1728]{1,0:T(8,128)(2,1)} %collective-permute-done.1), channel_id=1, source_target_pairs={{0,64},{64,128},{128,192},{192,256},{256,320},{320,384},{384,448},... | collective-permute-start | bytes 1327112 | tf_op jit(solution)/shard_map/ppermute | solution.py:18
  130.7 25.3 %collective-permute-start.10 = (bf16[128,1728]{1,0:T(8,128)(2,1)}, bf16[128,1728]{1,0:T(8,128)(2,1)S(1)}, u32[]{:S(2)}, u32[]{:S(2)}) collective-permute-start(bf16[128,1728]{1,0:T(8,128)(2,1)} %collective-permute-done.3), channel_id=1, source_target_pairs={{0,448},{64,0},{128,64},{192,128},{256,192},{320,256},{384,320},{4... | collective-permute-start | bytes 1327112 | tf_op jit(solution)/shard_map/ppermute | solution.py:18
  137.4 15.2 %collective-permute-start.12 = (bf16[128,1728]{1,0:T(8,128)(2,1)S(1)}, bf16[128,1728]{1,0:T(8,128)(2,1)S(1)}, u32[]{:S(2)}, u32[]{:S(2)}) collective-permute-start(bf16[128,1728]{1,0:T(8,128)(2,1)S(1)} %collective-permute-done.11), channel_id=1, source_target_pairs={{0,64},{64,128},{128,192},{192,256},{256,320},{320,384},{384,448},... | collective-permute-start | bytes 1327112 | tf_op jit(solution)/shard_map/ppermute | solution.py:18
  146.9 25.7 %all-to-all-start = ((bf16[8,2,64,432]{3,2,1,0:T(8,128)(2,1)}), bf16[8,2,64,432]{3,2,1,0:T(8,128)(2,1)S(1)}, u32[]{:S(2)}, u32[]{:S(2)}) async-start(bf16[8,2,64,432]{3,2,1,0:T(8,128)(2,1)} %copy.22), calls=%async_computation | async-start | bytes 2097152 | tf_op jit(solution)/shard_map/all_to_all | solution.py:50
  152.7 8.3 %collective-permute-start.13 = (bf16[64,1728]{1,0:T(8,128)(2,1)S(1)}, bf16[64,1728]{1,0:T(8,128)(2,1)S(1)}, u32[]{:S(2)}, u32[]{:S(2)}) collective-permute-start(bf16[64,1728]{1,0:T(8,128)(2,1)S(1)} %slice.79), channel_id=1, source_target_pairs={{0,64},{64,128},{128,192},{192,256},{256,320},{320,384},{384,448},... | collective-permute-start | bytes 663560 | tf_op jit(solution)/shard_map/ppermute | solution.py:18
  156.0 8.3 %collective-permute-start.14 = (bf16[64,1728]{1,0:T(8,128)(2,1)S(1)}, bf16[64,1728]{1,0:T(8,128)(2,1)S(1)}, u32[]{:S(2)}, u32[]{:S(2)}) collective-permute-start(bf16[64,1728]{1,0:T(8,128)(2,1)S(1)} %slice.80), channel_id=1, source_target_pairs={{0,448},{64,0},{128,64},{192,128},{256,192},{320,256},{384,320},{4... | collective-permute-start | bytes 663560 | tf_op jit(solution)/shard_map/ppermute | solution.py:18
  164.4 1.3 copy-start.1
  172.6 35.5 %all-to-all-start.3 = ((bf16[8,2,64,432]{3,2,1,0:T(8,128)(2,1)}), bf16[8,2,64,432]{3,2,1,0:T(8,128)(2,1)S(1)}, u32[]{:S(2)}, u32[]{:S(2)}) async-start(bf16[8,2,64,432]{3,2,1,0:T(8,128)(2,1)} %copy.30), calls=%async_computation.3 | async-start | bytes 2097152 | tf_op jit(solution)/shard_map/all_to_all | solution.py:50
  180.2 77.2 %all-gather.7.cloned.1.call-start = ((), (), s32[]{:S(2)}) async-start(), calls=%async_computation.4 | async-start | bytes 1769472 | tf_op jit(solution)/shard_map/all_gather | solution.py:44
  180.4 11.3 %collective-permute-start.5 = (bf16[2,64,432]{2,1,0:T(8,128)(2,1)S(1)}, bf16[2,64,432]{2,1,0:T(8,128)(2,1)S(1)}, u32[]{:S(2)}, u32[]{:S(2)}) collective-permute-start(bf16[2,64,432]{2,1,0:T(8,128)(2,1)S(1)} %convert_element_type.58), channel_id=1, source_target_pairs={{0,2},{2,0},{1,3},{3,1},{4,6},{6,4},{5,7},{7,5},{8,10},{10,8},{9,1... | collective-permute-start | bytes 331784 | tf_op jit(solution)/shard_map/ppermute | solution.py:22
  191.7 16.5 %collective-permute-start.6 = (bf16[64,432]{1,0:T(8,128)(2,1)S(1)}, bf16[64,432]{1,0:T(8,128)(2,1)S(1)}, u32[]{:S(2)}, u32[]{:S(2)}) collective-permute-start(bf16[64,432]{1,0:T(8,128)(2,1)S(1)} %slice_bitcast_fusion.2), channel_id=1, source_target_pairs={{0,16},{16,0},{32,48},{48,32},{1,17},{17,1},{33,49},{49,33},{2,18}... | collective-permute-start | bytes 165896 | tf_op jit(solution)/shard_map/ppermute | solution.py:22
  208.4 9.6 %collective-permute-start.15 = (bf16[2,64,432]{2,1,0:T(8,128)(2,1)S(1)}, bf16[2,64,432]{2,1,0:T(8,128)(2,1)S(1)}, u32[]{:S(2)}, u32[]{:S(2)}) collective-permute-start(bf16[2,64,432]{2,1,0:T(8,128)(2,1)S(1)} %convert_element_type.68), channel_id=1, source_target_pairs={{0,2},{2,0},{1,3},{3,1},{4,6},{6,4},{5,7},{7,5},{8,10},{10,8},{9,1... | collective-permute-start | bytes 331784 | tf_op jit(solution)/shard_map/ppermute | solution.py:22
  218.1 22.3 %collective-permute-start.16 = (bf16[64,432]{1,0:T(8,128)(2,1)S(1)}, bf16[64,432]{1,0:T(8,128)(2,1)S(1)}, u32[]{:S(2)}, u32[]{:S(2)}) collective-permute-start(bf16[64,432]{1,0:T(8,128)(2,1)S(1)} %slice_bitcast_fusion), channel_id=1, source_target_pairs={{0,16},{16,0},{32,48},{48,32},{1,17},{17,1},{33,49},{49,33},{2,18}... | collective-permute-start | bytes 165896 | tf_op jit(solution)/shard_map/ppermute | solution.py:22
  230.2 25.4 %collective-permute-start.7 = (bf16[4,2,64,432]{3,2,1,0:T(8,128)(2,1)S(1)}, bf16[4,2,64,432]{3,2,1,0:T(8,128)(2,1)S(1)}, u32[]{:S(2)}, u32[]{:S(2)}) collective-permute-start(bf16[4,2,64,432]{3,2,1,0:T(8,128)(2,1)S(1)} %bitcast.81), channel_id=1, source_target_pairs={{0,1},{1,0},{2,3},{3,2},{4,5},{5,4},{6,7},{7,6},{8,9},{9,8},{10,11... | collective-permute-start | bytes 1327112 | tf_op jit(solution)/shard_map/ppermute | solution.py:22
  251.1 5.8 %collective-permute-start.17 = (bf16[4,2,64,432]{3,2,1,0:T(8,128)(2,1)S(1)}, bf16[4,2,64,432]{3,2,1,0:T(8,128)(2,1)S(1)}, u32[]{:S(2)}, u32[]{:S(2)}) collective-permute-start(bf16[4,2,64,432]{3,2,1,0:T(8,128)(2,1)S(1)} %bitcast.83), channel_id=1, source_target_pairs={{0,1},{1,0},{2,3},{3,2},{4,5},{5,4},{6,7},{7,6},{8,9},{9,8},{10,11... | collective-permute-start | bytes 1327112 | tf_op jit(solution)/shard_map/ppermute | solution.py:22
Sparse Core Ops, SparseCore 0:
  208.3 39.2 all-gather.6

commit v2 on v0

v2 whole, which is shorter than its diff:
```python
import jax
import jax.numpy as jnp
from jax import lax
from jax.experimental import pallas as pl
from jax.experimental.pallas import tpu as pltpu
from jax.sharding import Mesh, PartitionSpec as P

F32, BF16 = jnp.float32, jnp.bfloat16
SPLIT = (8, 2, 2, 4, 2, 2)
AXES = ("y", "zq", "zp", "x", "zh", "core")
TOK, COL = ("y", "zq", "zp"), ("x", "zh", "core")


def dot(a, b):
    return jnp.dot(a, b, preferred_element_type=F32)


def tie(values, earlier=()):
    n = len(values)
    whole = pl.BlockSpec(memory_space=pl.ANY)
    return pl.pallas_call(
        lambda *refs: None,
        out_shape=[jax.ShapeDtypeStruct(v.shape, v.dtype) for v in values],
        in_specs=[whole] * (n + len(earlier)),
        out_specs=[whole] * n,
        input_output_aliases={i: i for i in range(n)},
    )(*values, *earlier)


def shift(value, axis, by):
    n = lax.axis_size(axis)
    return lax.ppermute(value, axis, [(i, (i + by) % n) for i in range(n)])


def swap(value, axis):
    return lax.ppermute(value, axis, [(0, 1), (1, 0)])


def ordered(axis, mine, other):
    first = lax.axis_index(axis) == 0
    return jnp.stack([jnp.where(first, mine, other), jnp.where(first, other, mine)])


def spread(value, axis):
    parts = [value] + [lax.ppermute(value, axis, [(i, i ^ k) for i in range(4)]) for k in (1, 2, 3)]
    me = lax.axis_index(axis)
    odd, high = me % 2 == 1, me >= 2
    parts = [jnp.where(odd, parts[s ^ 1], parts[s]) for s in range(4)]
    return jnp.stack([jnp.where(high, parts[s ^ 2], parts[s]) for s in range(4)])


def partial_kernel(zp_ref, all_ref, own_ref, low_ref, high_ref, out_ref, rows, bases, outs, sems):
    n, low = rows.shape[1], low_ref.shape[0]
    loads = [
        (own_ref, bases.at[0]),
        (all_ref.at[pl.ds(0, n)], rows.at[0]),
        (low_ref, bases.at[1, pl.ds(0, low)]),
        (high_ref, bases.at[1, pl.ds(low, high_ref.shape[0])]),
        (all_ref.at[pl.ds(n, n)], rows.at[1]),
    ]
    loads = [pltpu.make_async_copy(a, b, sems.at[i]) for i, (a, b) in enumerate(loads)]
    for load in loads:
        load.start()
    zp = zp_ref[0]
    stores = []
    for h, which, needed in ((0, 0, loads[:2]), (0, 1, loads[2:4]), (1, 0, loads[4:]), (1, 1, ())):
        for load in needed:
            load.wait()
        part = lax.dot_general(
            bases[which], rows[h], (((1,), (1,)), ((), ())), preferred_element_type=F32
        ).astype(BF16)
        at, width = len(stores), outs.shape[3]
        for i in range(4):
            outs[at, i] = part[:, i * width : (i + 1) * width]
        place = zp if which == 0 else 1 - zp
        stores.append(
            pltpu.make_async_copy(outs.at[at], out_ref.at[pl.ds(place * 8 + h * 4, 4)], sems.at[5 + at])
        )
        stores[-1].start()
    for store in stores:
        store.wait()


def partial_sums(gathered, own, other):
    rows, feats = gathered.shape[0] // 2, gathered.shape[1]
    outs = own.shape[0]
    whole = pl.BlockSpec(memory_space=pl.ANY)
    return pl.pallas_call(
        partial_kernel,
        out_shape=jax.ShapeDtypeStruct((16, outs, rows // 4), BF16),
        in_specs=[pl.BlockSpec(memory_space=pltpu.SMEM)] + [whole] * 4,
        out_specs=whole,
        scratch_shapes=[
            pltpu.VMEM((2, rows, feats), BF16),
            pltpu.VMEM((2, outs, feats), BF16),
            pltpu.VMEM((4, 4, outs, rows // 4), BF16),
            pltpu.SemaphoreType.DMA((9,)),
        ],
        compiler_params=pltpu.CompilerParams(vmem_limit_bytes=60 * 2**20),
        cost_estimate=pl.CostEstimate(
            flops=8 * rows * feats * outs, bytes_accessed=4 * rows * feats, transcendentals=0
        ),
    )(lax.axis_index("zp").reshape(1), gathered, own, *other)


def on_device(grads, acts, grad_basis, act_basis):
    half = grads.shape[0]
    quarter, feats = acts.shape[0] // 4, acts.shape[1]
    cols = act_basis.shape[1]
    own_basis = grad_basis.T

    other = swap(grads, "zq")
    act = lax.all_to_all(acts.reshape(4, quarter, feats), ("zq", "zp"), 0, 0)
    other, act = tie([other, act])
    gathered = lax.all_gather(jnp.concatenate([grads, other], 0), "y", axis=0, tiled=True)

    act = ordered("zh", act, swap(act, "zh"))
    cut = 256
    send, act, act_basis = tie([own_basis[:cut], act, act_basis])
    other_basis = [swap(send, "zp")]
    basis = spread(act_basis, ("zq", "zp"))
    act = spread(act, "x")
    send, act = tie([own_basis[cut:], act], other_basis)
    other_basis.append(swap(send, "zp"))
    act = ordered("core", act, swap(act, "core"))
    act = act.reshape(16, 4, quarter, feats)
    rot = sum(dot(act[:, s].reshape(-1, feats), basis[s]) for s in range(4))
    rot = rot.astype(BF16).reshape(2, 8, quarter, cols).transpose(1, 0, 2, 3)
    rot = lax.all_to_all(rot, "y", 0, 0)
    (rot,) = tie([rot], other_basis)
    rot = rot.astype(F32).sum(0)
    sq = spread((rot * rot).astype(BF16), ("zq", "zp"))
    sq = sq.reshape(2, 2, 2, quarter, cols)
    first = lax.axis_index("zq") == 0
    sq = jnp.stack([jnp.where(first, sq[:, :, 0], sq[:, :, 1]), jnp.where(first, sq[:, :, 1], sq[:, :, 0])], 1)
    sq = sq.reshape(-1, cols)
    sq_act = lax.all_gather(sq, "y", axis=0, tiled=True)

    part = partial_sums(gathered, own_basis, other_basis)
    part = lax.all_to_all(part, ("zp", "core", "x"), 0, 0)
    part = part.transpose(0, 2, 1).reshape(2, 8, 2 * half, -1).astype(F32).sum(1)
    rot = part + swap(part.astype(BF16), "zh").astype(F32)
    sq = lax.all_gather((rot * rot).astype(BF16), "x", axis=0)
    mine, there = (v.reshape(-1, v.shape[-1]) for v in (sq, swap(sq, "core")))
    tokens = sq_act.shape[0] // 2
    core = lax.axis_index("core")
    total = sum(
        lax.dot_general(
            g,
            lax.dynamic_slice_in_dim(sq_act, at * tokens, tokens, 0),
            (((0,), (0,)), ((), ())),
            preferred_element_type=F32,
        )
        for g, at in ((mine, core), (there, 1 - core))
    )
    return total / F32(2 * tokens)


def solution(mesh):
    return jax.shard_map(
        on_device,
        mesh=Mesh(mesh.devices.reshape(SPLIT), AXES),
        in_specs=(P(TOK, COL), P(COL, TOK), P(COL, TOK), P(TOK, COL)),
        out_specs=P(TOK, COL),
        check_vma=False,
    )
```

time: 799 us -> 195 us (0.24)
  the two profiles are of different devices: /device:TPU:48 before, /device:TPU:2 now
where the time goes in v2:
time: 195 us; the launch traced here: 194 us
  starting transfers between devices  74.5 us (38%)
  waiting for transfers between devices  48.8 us (25%)
  blocking collectives  24.9 us (13%)
  between operations  13.8 us (7%)
  local copies, waits for them, and re-layouts  12.1 us (6%)
  other arithmetic  8.18 us (4%)
  Pallas kernels  6.61 us (3%)
  matrix products  5.43 us (3%)
    ppermute x7, starting transfers between devices, swap(): return lax.ppermute(value, axis, [(0, 1), (1, 0)])  31.1 us
    ppermute x9, starting transfers between devices, spread(): lax.ppermute(value, axis, [(i, i ^ k) for i in range(4)])  30.9 us
    ppermute x9, waiting for transfers between devices, spread(): lax.ppermute(value, axis, [(i, i ^ k) for i in range(4)])  20.7 us
    ppermute x7, waiting for transfers between devices, swap(): return lax.ppermute(value, axis, [(0, 1), (1, 0)])  14.1 us
    all_gather x1, blocking collectives, on_device(): sq = lax.all_gather((rot * rot).astype(BF16), 'x', axis=0)  13.6 us
    all_gather x1, waiting for transfers between devices, on_device(): sq_act = lax.all_gather(sq, 'y', axis=0, tiled=True)  11.6 us
    all_to_all x1, blocking collectives, on_device(): act = lax.all_to_all(acts.reshape(4, quarter, feats), ('zq', 'zp'), 0, 0)  11.3 us
    all_to_all x1, starting transfers between devices, on_device(): rot = lax.all_to_all(rot, 'y', 0, 0)  7.1 us
  transfers between devices with their start and end apart: 20, of which 10 were waited for; matrix products, arithmetic and copies ran while one was open for 8% of the time, Pallas kernels for 3%

profile of v2, /device:TPU:2, one launch (start us, length us, event | category | flops | bytes accessed | tf_op | source)
XLA Modules:
  0.0 194.3 jit_solution(18121485386938053787)
XLA Ops:
  6.5 1.7 copy.67.refs_2_
  8.2 6.1 %collective-permute-start = (bf16[64,1728]{1,0:T(8,128)(2,1)}, bf16[64,1728]{1,0:T(8,128)(2,1)S(1)}, u32[]{:S(2)}, u32[]{:S(2)}) collective-permute-start(bf16[64,1728]{1,0:T(8,128)(2,1)} %param.4), channel_id=1, source_target_pairs={{0,32},{32,0},{1,33},{33,1},{2,34},{34,2},{3,35},{35,3},{4,36},{36... | collective-permute-start | bytes 663560 | tf_op jit(solution)/shard_map/ppermute | solution.py:36
  14.3 0.9 copy.38
  15.2 11.3 %all_to_all.15.refs_1_ = bf16[4,32,160]{2,1,0:T(8,128)(2,1)} all-to-all(bf16[4,32,160]{2,1,0:T(8,128)(2,1)S(1)} %bitcast.81), channel_id=1, replica_groups=mesh['y'=8,'zq'=2,'zp'=2,'x'=4,'zh'=2,'core'=2] {'zq','zp'}, dimensions={0} | all-to-all | bytes 81920 | tf_op jit(solution)/shard_map/all_to_all | solution.py:113
  26.5 0.7 copy-done.4
  27.2 1.9 pad_maximum_fusion.2
  29.2 9.4 %collective-permute-start.1 = (bf16[4,32,160]{2,1,0:T(8,128)(2,1)}, bf16[4,32,160]{2,1,0:T(8,128)(2,1)S(1)}, u32[]{:S(2)}, u32[]{:S(2)}) collective-permute-start(bf16[4,32,160]{2,1,0:T(8,128)(2,1)} %get-tuple-element.13), channel_id=1, source_target_pairs={{0,2},{2,0},{1,3},{3,1},{4,6},{6,4},{5,7},{7,5},{8,10},{10,8},{9,1... | collective-permute-start | bytes 122888 | tf_op jit(solution)/shard_map/ppermute | solution.py:36
  38.5 1.0 slice.34.refs_0_
  39.5 1.5 collective-permute-done.1
  41.8 1.6 copy.39
  43.4 2.2 %collective-permute-start.2 = (bf16[256,1728]{0,1:T(8,128)(2,1)S(1)}, bf16[256,1728]{0,1:T(8,128)(2,1)S(1)}, u32[]{:S(2)}, u32[]{:S(2)}) collective-permute-start(bf16[256,1728]{0,1:T(8,128)(2,1)S(1)} %copy.39), channel_id=1, source_target_pairs={{0,16},{16,0},{1,17},{17,1},{2,18},{18,2},{3,19},{19,3},{4,20},{20... | collective-permute-start | bytes 2654216 | tf_op jit(solution)/shard_map/ppermute | solution.py:36
  45.6 3.4 %collective-permute-start.3 = (bf16[2,4,32,160]{3,2,1,0:T(8,128)(2,1)S(1)}, bf16[2,4,32,160]{3,2,1,0:T(8,128)(2,1)}, u32[]{:S(2)}, u32[]{:S(2)}) collective-permute-start(bf16[2,4,32,160]{3,2,1,0:T(8,128)(2,1)S(1)} %copy-done.3), channel_id=1, source_target_pairs={{0,12},{4,8},{8,4},{12,0},{1,13},{5,9},{9,5},{13,1},{2,14},{6,10},... | collective-permute-start | bytes 245768 | tf_op jit(solution)/shard_map/ppermute | solution.py:45
  49.0 3.0 %collective-permute-start.4 = (bf16[2,4,32,160]{3,2,1,0:T(8,128)(2,1)S(1)}, bf16[2,4,32,160]{3,2,1,0:T(8,128)(2,1)}, u32[]{:S(2)}, u32[]{:S(2)}) collective-permute-start(bf16[2,4,32,160]{3,2,1,0:T(8,128)(2,1)S(1)} %copy-done.3), channel_id=1, source_target_pairs={{0,8},{4,12},{8,0},{12,4},{1,9},{5,13},{9,1},{13,5},{2,10},{6,14},... | collective-permute-start | bytes 245768 | tf_op jit(solution)/shard_map/ppermute | solution.py:45
  52.0 3.4 %collective-permute-start.5 = (bf16[2,4,32,160]{3,2,1,0:T(8,128)(2,1)S(1)}, bf16[2,4,32,160]{3,2,1,0:T(8,128)(2,1)}, u32[]{:S(2)}, u32[]{:S(2)}) collective-permute-start(bf16[2,4,32,160]{3,2,1,0:T(8,128)(2,1)S(1)} %copy-done.3), channel_id=1, source_target_pairs={{0,4},{4,0},{8,12},{12,8},{1,5},{5,1},{9,13},{13,9},{2,6},{6,2},{1... | collective-permute-start | bytes 245768 | tf_op jit(solution)/shard_map/ppermute | solution.py:45
  55.4 0.9 slice.35.refs_0_
  56.3 2.2 %collective-permute-done.4 = bf16[2,4,32,160]{3,2,1,0:T(8,128)(2,1)} collective-permute-done((bf16[2,4,32,160]{3,2,1,0:T(8,128)(2,1)S(1)}, bf16[2,4,32,160]{3,2,1,0:T(8,128)(2,1)}, u32[]{:S(2)}, u32[]{:S(2)}) %collective-permute-start.4) | collective-permute-done | bytes 81952 | tf_op jit(solution)/shard_map/ppermute | solution.py:45
  59.1 1.1 select_bitcast_fusion.5
  60.2 0.9 pad_maximum_fusion.1.refs_1_
  61.1 3.7 %collective-permute-done.2 = bf16[256,1728]{0,1:T(8,128)(2,1)S(1)} collective-permute-done((bf16[256,1728]{0,1:T(8,128)(2,1)S(1)}, bf16[256,1728]{0,1:T(8,128)(2,1)S(1)}, u32[]{:S(2)}, u32[]{:S(2)}) %collective-permute-start.2) | collective-permute-done | bytes 884768 | tf_op jit(solution)/shard_map/ppermute | solution.py:36
  64.8 1.4 copy.41.refs_2_.low_ref.refs_1_
  66.2 1.9 collective-permute-start.8
  68.2 5.4 %collective-permute-start.10 = (bf16[160,320]{1,0:T(8,128)(2,1)S(1)}, bf16[160,320]{1,0:T(8,128)(2,1)S(1)}, u32[]{:S(2)}, u32[]{:S(2)}) collective-permute-start(bf16[160,320]{1,0:T(8,128)(2,1)S(1)} %copy-done), channel_id=1, source_target_pairs={{0,32},{16,48},{32,0},{48,16},{1,33},{17,49},{33,1},{49,17},{2,34}... | collective-permute-start | bytes 307208 | tf_op jit(solution)/shard_map/ppermute | solution.py:45
  73.6 3.6 %collective-permute-start.11 = (bf16[160,320]{1,0:T(8,128)(2,1)S(1)}, bf16[160,320]{1,0:T(8,128)(2,1)S(1)}, u32[]{:S(2)}, u32[]{:S(2)}) collective-permute-start(bf16[160,320]{1,0:T(8,128)(2,1)S(1)} %copy-done), channel_id=1, source_target_pairs={{0,16},{16,0},{32,48},{48,32},{1,17},{17,1},{33,49},{49,33},{2,18}... | collective-permute-start | bytes 307208 | tf_op jit(solution)/shard_map/ppermute | solution.py:45
  77.2 1.9 collective-permute-start.9
  79.2 2.5 %collective-permute-start.6 = (bf16[176,1728]{1,0:T(8,128)(2,1)}, bf16[176,1728]{1,0:T(8,128)(2,1)S(1)}, u32[]{:S(2)}, u32[]{:S(2)}) collective-permute-start(bf16[176,1728]{1,0:T(8,128)(2,1)} %get-tuple-element.16), channel_id=1, source_target_pairs={{0,16},{16,0},{1,17},{17,1},{2,18},{18,2},{3,19},{19,3},{4,20},{20... | collective-permute-start | bytes 1824776 | tf_op jit(solution)/shard_map/ppermute | solution.py:36
  81.7 1.1 select_bitcast_fusion.1
  83.1 3.6 %collective-permute-done.9 = bf16[160,320]{1,0:T(8,128)(2,1)S(1)} collective-permute-done((bf16[160,320]{1,0:T(8,128)(2,1)S(1)}, bf16[160,320]{1,0:T(8,128)(2,1)S(1)}, u32[]{:S(2)}, u32[]{:S(2)}) %collective-permute-start.9) | collective-permute-done | bytes 102432 | tf_op jit(solution)/shard_map/ppermute | solution.py:45
  88.1 0.8 copy.57
  89.0 7.1 %all-to-all-start.2 = ((bf16[8,2,32,320]{3,2,1,0:T(8,128)(2,1)}), bf16[8,2,32,320]{3,2,1,0:T(8,128)(2,1)S(1)}, u32[]{:S(2)}, u32[]{:S(2)}) async-start(bf16[8,2,32,320]{3,2,1,0:T(8,128)(2,1)} %bitcast.68), calls=%async_computation.2 | async-start | bytes 786432 | tf_op jit(solution)/shard_map/all_to_all | solution.py:129
  96.1 3.7 %collective-permute-done.6.high_ref.refs_2_ = bf16[176,1728]{1,0:T(8,128)(2,1)S(1)} collective-permute-done((bf16[176,1728]{1,0:T(8,128)(2,1)}, bf16[176,1728]{1,0:T(8,128)(2,1)S(1)}, u32[]{:S(2)}, u32[]{:S(2)}) %collective-permute-start.6) | collective-permute-done | bytes 608288 | tf_op jit(solution)/shard_map/ppermute | solution.py:36
  99.7 0.8 copy-done.5
  100.5 6.6 %shard_map.49 = bf16[16,432,128]{2,1,0:T(8,128)(2,1)} custom-call(s32[1]{0:T(128)} %bitcast.zp_ref, bf16[1024,1728]{1,0:T(8,128)(2,1)} %all-gather.4.cloned.1.call-done.all_ref, bf16[432,1728]{1,0:T(8,128)(2,1)} %bitcast.72, bf16[256,1728]{1,0:T(8,128)(2,1)} %copy.41.refs_2_.low_ref.refs_1_, bf16[176,1728]{1,0:T(8,128)(2,1)} %copy-done.5), custom_call_target="tpu_custom_call" | custom-call | flops 3057647616 | bytes 3538944 | tf_op jit(solution)/shard_map/pallas_call | solution.py:88
  107.2 2.3 %all-to-all-done.2.refs_0_ = bf16[8,2,32,320]{3,2,1,0:T(8,128)(2,1)S(1)} async-done(((bf16[8,2,32,320]{3,2,1,0:T(8,128)(2,1)}), bf16[8,2,32,320]{3,2,1,0:T(8,128)(2,1)S(1)}, u32[]{:S(2)}, u32[]{:S(2)}) %all-to-all-start.2) | async-done | bytes 327712 | tf_op jit(solution)/shard_map/all_to_all | solution.py:129
  109.5 0.7 copy-done.1
  110.3 5.3 %all-to-all-start.1 = ((bf16[16,432,128]{2,1,0:T(8,128)(2,1)}), bf16[16,432,128]{2,1,0:T(8,128)(2,1)S(1)}, u32[]{:S(2)}, u32[]{:S(2)}) async-start(bf16[16,432,128]{2,1,0:T(8,128)(2,1)} %shard_map.49), calls=%async_computation.1 | async-start | bytes 3538944 | tf_op jit(solution)/shard_map/all_to_all | solution.py:140
  115.6 1.1 convert_reduce_fusion
  116.7 5.3 %collective-permute-start.12 = (bf16[2,32,320]{2,1,0:T(8,128)(2,1)S(1)}, bf16[2,32,320]{2,1,0:T(8,128)(2,1)S(1)}, u32[]{:S(2)}, u32[]{:S(2)}) collective-permute-start(bf16[2,32,320]{2,1,0:T(8,128)(2,1)S(1)} %multiply_convert_fusion.1), channel_id=1, source_target_pairs={{0,48},{16,32},{32,16},{48,0},{1,49},{17,33},{33,17},{49,1},{2,50}... | collective-permute-start | bytes 122888 | tf_op jit(solution)/shard_map/ppermute | solution.py:45
  122.0 1.9 collective-permute-start.13
  123.9 2.9 %collective-permute-start.14 = (bf16[2,32,320]{2,1,0:T(8,128)(2,1)S(1)}, bf16[2,32,320]{2,1,0:T(8,128)(2,1)S(1)}, u32[]{:S(2)}, u32[]{:S(2)}) collective-permute-start(bf16[2,32,320]{2,1,0:T(8,128)(2,1)S(1)} %multiply_convert_fusion.1), channel_id=1, source_target_pairs={{0,16},{16,0},{32,48},{48,32},{1,17},{17,1},{33,49},{49,33},{2,18}... | collective-permute-start | bytes 122888 | tf_op jit(solution)/shard_map/ppermute | solution.py:45
  126.8 14.3 %collective-permute-done.12 = bf16[2,32,320]{2,1,0:T(8,128)(2,1)S(1)} collective-permute-done((bf16[2,32,320]{2,1,0:T(8,128)(2,1)S(1)}, bf16[2,32,320]{2,1,0:T(8,128)(2,1)S(1)}, u32[]{:S(2)}, u32[]{:S(2)}) %collective-permute-start.12) | collective-permute-done | bytes 40992 | tf_op jit(solution)/shard_map/ppermute | solution.py:45
  141.3 0.7 pad_maximum_fusion.4
  142.3 7.2 %collective-permute-start.7 = (bf16[2,128,432]{1,2,0:T(8,128)(2,1)S(1)}, bf16[2,128,432]{1,2,0:T(8,128)(2,1)S(1)}, u32[]{:S(2)}, u32[]{:S(2)}) collective-permute-start(bf16[2,128,432]{1,2,0:T(8,128)(2,1)S(1)} %convert_element_type.30), channel_id=1, source_target_pairs={{0,2},{2,0},{1,3},{3,1},{4,6},{6,4},{5,7},{7,5},{8,10},{10,8},{9,1... | collective-permute-start | bytes 663560 | tf_op jit(solution)/shard_map/ppermute | solution.py:36
  149.5 5.2 %collective-permute-done.7 = bf16[2,128,432]{1,2,0:T(8,128)(2,1)S(1)} collective-permute-done((bf16[2,128,432]{1,2,0:T(8,128)(2,1)S(1)}, bf16[2,128,432]{1,2,0:T(8,128)(2,1)S(1)}, u32[]{:S(2)}, u32[]{:S(2)}) %collective-permute-start.7) | collective-permute-done | bytes 221216 | tf_op jit(solution)/shard_map/ppermute | solution.py:36
  154.8 13.6 %all-gather = bf16[8,128,432]{1,2,0:T(8,128)(2,1)S(1)} all-gather(bf16[2,128,432]{1,2,0:T(8,128)(2,1)S(1)} %multiply_convert_fusion), channel_id=2, replica_groups=mesh['y'=8,'zq'=2,'zp'=2,'x'=4,'zh'=2,'core'=2] {'x'}, dimensions={0}, use_global_device_ids=true | all-gather | bytes 1105920 | tf_op jit(solution)/shard_map/all_gather | solution.py:143
  168.4 1.9 collective-permute-start.15
  170.3 11.6 %all-gather.6.cloned.1.call-done = bf16[2048,320]{1,0:T(8,128)(2,1)} async-done(((bf16[256,320]{1,0:T(8,128)(2,1)}), bf16[2048,320]{1,0:T(8,128)(2,1)}) %all-gather.6.cloned.1.call-update) | async-done | bytes 1310736 | tf_op jit(solution)/shard_map/all_gather | solution.py:137
  181.9 1.7 fusion.4
  184.9 2.5 %fusion = f32[432,320]{0,1:T(8,128)} fusion(f32[432,320]{0,1:T(8,128)S(1)} %fusion.4, bf16[1024,432]{0,1:T(8,128)(2,1)S(1)} %reshape.72, bf16[2048,320]{1,0:T(8,128)(2,1)} %all-gather.6.cloned.1.call-done, s32[]{:T(128)S(6)} %select_n.233), kind=kOutput, calls=%fused_computation.2 | convolution fusion | flops 283392000 | bytes 2777092 | tf_op jit(solution)/shard_map/dot_general | solution.py:148
  (48 shorter events, 4.9 us)
Async XLA Ops:
  6.5 32.0 %copy-start.2 = (bf16[1728,432]{0,1:T(8,128)(2,1)S(1)}, bf16[1728,432]{0,1:T(8,128)(2,1)}, u32[]{:S(2)}) copy-start(bf16[1728,432]{0,1:T(8,128)(2,1)} %param.6) | copy-start | bytes 4478980
  6.5 93.2 %all-gather.4.cloned.1.call-start = ((), (), s32[]{:S(2)}) async-start(), calls=%async_computation.3 | async-start | bytes 4128768 | tf_op jit(solution)/shard_map/all_gather | solution.py:115
  8.2 18.3 %collective-permute-start = (bf16[64,1728]{1,0:T(8,128)(2,1)}, bf16[64,1728]{1,0:T(8,128)(2,1)S(1)}, u32[]{:S(2)}, u32[]{:S(2)}) collective-permute-start(bf16[64,1728]{1,0:T(8,128)(2,1)} %param.4), channel_id=1, source_target_pairs={{0,32},{32,0},{1,33},{33,1},{2,34},{34,2},{3,35},{35,3},{4,36},{36... | collective-permute-start | bytes 663560 | tf_op jit(solution)/shard_map/ppermute | solution.py:36
  26.5 0.7 copy-start.4
  27.2 13.8 %copy-start.6 = (bf16[4,32,160]{2,1,0:T(8,128)(2,1)S(1)}, bf16[4,32,160]{2,1,0:T(8,128)(2,1)}, u32[]{:S(2)}) copy-start(bf16[4,32,160]{2,1,0:T(8,128)(2,1)} %get-tuple-element.13) | copy-start | bytes 122884
  29.2 11.9 %collective-permute-start.1 = (bf16[4,32,160]{2,1,0:T(8,128)(2,1)}, bf16[4,32,160]{2,1,0:T(8,128)(2,1)S(1)}, u32[]{:S(2)}, u32[]{:S(2)}) collective-permute-start(bf16[4,32,160]{2,1,0:T(8,128)(2,1)} %get-tuple-element.13), channel_id=1, source_target_pairs={{0,2},{2,0},{1,3},{3,1},{4,6},{6,4},{5,7},{7,5},{8,10},{10,8},{9,1... | collective-permute-start | bytes 122888 | tf_op jit(solution)/shard_map/ppermute | solution.py:36
  41.8 3.8 %copy-start.3 = (bf16[2,4,32,160]{3,2,1,0:T(8,128)(2,1)S(1)}, bf16[2,4,32,160]{3,2,1,0:T(8,128)(2,1)}, u32[]{:S(2)}) copy-start(bf16[2,4,32,160]{3,2,1,0:T(8,128)(2,1)} %get-tuple-element.15) | copy-start | bytes 245764
  43.4 21.5 %collective-permute-start.2 = (bf16[256,1728]{0,1:T(8,128)(2,1)S(1)}, bf16[256,1728]{0,1:T(8,128)(2,1)S(1)}, u32[]{:S(2)}, u32[]{:S(2)}) collective-permute-start(bf16[256,1728]{0,1:T(8,128)(2,1)S(1)} %copy.39), channel_id=1, source_target_pairs={{0,16},{16,0},{1,17},{17,1},{2,18},{18,2},{3,19},{19,3},{4,20},{20... | collective-permute-start | bytes 2654216 | tf_op jit(solution)/shard_map/ppermute | solution.py:36
  45.6 10.7 %collective-permute-start.3 = (bf16[2,4,32,160]{3,2,1,0:T(8,128)(2,1)S(1)}, bf16[2,4,32,160]{3,2,1,0:T(8,128)(2,1)}, u32[]{:S(2)}, u32[]{:S(2)}) collective-permute-start(bf16[2,4,32,160]{3,2,1,0:T(8,128)(2,1)S(1)} %copy-done.3), channel_id=1, source_target_pairs={{0,12},{4,8},{8,4},{12,0},{1,13},{5,9},{9,5},{13,1},{2,14},{6,10},... | collective-permute-start | bytes 245768 | tf_op jit(solution)/shard_map/ppermute | solution.py:45
  49.0 9.5 %collective-permute-start.4 = (bf16[2,4,32,160]{3,2,1,0:T(8,128)(2,1)S(1)}, bf16[2,4,32,160]{3,2,1,0:T(8,128)(2,1)}, u32[]{:S(2)}, u32[]{:S(2)}) collective-permute-start(bf16[2,4,32,160]{3,2,1,0:T(8,128)(2,1)S(1)} %copy-done.3), channel_id=1, source_target_pairs={{0,8},{4,12},{8,0},{12,4},{1,9},{5,13},{9,1},{13,5},{2,10},{6,14},... | collective-permute-start | bytes 245768 | tf_op jit(solution)/shard_map/ppermute | solution.py:45
  52.0 7.1 %collective-permute-start.5 = (bf16[2,4,32,160]{3,2,1,0:T(8,128)(2,1)S(1)}, bf16[2,4,32,160]{3,2,1,0:T(8,128)(2,1)}, u32[]{:S(2)}, u32[]{:S(2)}) collective-permute-start(bf16[2,4,32,160]{3,2,1,0:T(8,128)(2,1)S(1)} %copy-done.3), channel_id=1, source_target_pairs={{0,4},{4,0},{8,12},{12,8},{1,5},{5,1},{9,13},{13,9},{2,6},{6,2},{1... | collective-permute-start | bytes 245768 | tf_op jit(solution)/shard_map/ppermute | solution.py:45
  61.1 7.0 %copy-start = (bf16[160,320]{1,0:T(8,128)(2,1)S(1)}, bf16[160,320]{1,0:T(8,128)(2,1)}, u32[]{:S(2)}) copy-start(bf16[160,320]{1,0:T(8,128)(2,1)} %get-tuple-element.18) | copy-start | bytes 307204
  66.2 15.4 %collective-permute-start.8 = (bf16[4,2,4,32,160]{4,3,2,1,0:T(8,128)(2,1)}, bf16[4,2,4,32,160]{4,3,2,1,0:T(8,128)(2,1)S(1)}, u32[]{:S(2)}, u32[]{:S(2)}) collective-permute-start(bf16[4,2,4,32,160]{4,3,2,1,0:T(8,128)(2,1)} %get-tuple-element.17), channel_id=1, source_target_pairs={{0,1},{1,0},{2,3},{3,2},{4,5},{5,4},{6,7},{7,6},{8,9},{9,8},{10,11... | collective-permute-start | bytes 983048 | tf_op jit(solution)/shard_map/ppermute | solution.py:36
  68.2 14.9 %collective-permute-start.10 = (bf16[160,320]{1,0:T(8,128)(2,1)S(1)}, bf16[160,320]{1,0:T(8,128)(2,1)S(1)}, u32[]{:S(2)}, u32[]{:S(2)}) collective-permute-start(bf16[160,320]{1,0:T(8,128)(2,1)S(1)} %copy-done), channel_id=1, source_target_pairs={{0,32},{16,48},{32,0},{48,16},{1,33},{17,49},{33,1},{49,17},{2,34}... | collective-permute-start | bytes 307208 | tf_op jit(solution)/shard_map/ppermute | solution.py:45
  73.6 9.5 %collective-permute-start.11 = (bf16[160,320]{1,0:T(8,128)(2,1)S(1)}, bf16[160,320]{1,0:T(8,128)(2,1)S(1)}, u32[]{:S(2)}, u32[]{:S(2)}) collective-permute-start(bf16[160,320]{1,0:T(8,128)(2,1)S(1)} %copy-done), channel_id=1, source_target_pairs={{0,16},{16,0},{32,48},{48,32},{1,17},{17,1},{33,49},{49,33},{2,18}... | collective-permute-start | bytes 307208 | tf_op jit(solution)/shard_map/ppermute | solution.py:45
  77.2 9.4 %collective-permute-start.9 = (bf16[160,320]{1,0:T(8,128)(2,1)S(1)}, bf16[160,320]{1,0:T(8,128)(2,1)S(1)}, u32[]{:S(2)}, u32[]{:S(2)}) collective-permute-start(bf16[160,320]{1,0:T(8,128)(2,1)S(1)} %copy-done), channel_id=1, source_target_pairs={{0,48},{16,32},{32,16},{48,0},{1,49},{17,33},{33,17},{49,1},{2,50}... | collective-permute-start | bytes 307208 | tf_op jit(solution)/shard_map/ppermute | solution.py:45
  79.2 20.5 %collective-permute-start.6 = (bf16[176,1728]{1,0:T(8,128)(2,1)}, bf16[176,1728]{1,0:T(8,128)(2,1)S(1)}, u32[]{:S(2)}, u32[]{:S(2)}) collective-permute-start(bf16[176,1728]{1,0:T(8,128)(2,1)} %get-tuple-element.16), channel_id=1, source_target_pairs={{0,16},{16,0},{1,17},{17,1},{2,18},{18,2},{3,19},{19,3},{4,20},{20... | collective-permute-start | bytes 1824776 | tf_op jit(solution)/shard_map/ppermute | solution.py:36
  89.0 20.6 %all-to-all-start.2 = ((bf16[8,2,32,320]{3,2,1,0:T(8,128)(2,1)}), bf16[8,2,32,320]{3,2,1,0:T(8,128)(2,1)S(1)}, u32[]{:S(2)}, u32[]{:S(2)}) async-start(bf16[8,2,32,320]{3,2,1,0:T(8,128)(2,1)} %bitcast.68), calls=%async_computation.2 | async-start | bytes 786432 | tf_op jit(solution)/shard_map/all_to_all | solution.py:129
  99.7 0.8 copy-start.5
  109.5 0.7 copy-start.1
  110.3 31.8 %all-to-all-start.1 = ((bf16[16,432,128]{2,1,0:T(8,128)(2,1)}), bf16[16,432,128]{2,1,0:T(8,128)(2,1)S(1)}, u32[]{:S(2)}, u32[]{:S(2)}) async-start(bf16[16,432,128]{2,1,0:T(8,128)(2,1)} %shard_map.49), calls=%async_computation.1 | async-start | bytes 3538944 | tf_op jit(solution)/shard_map/all_to_all | solution.py:140
  115.6 66.4 %all-gather.6.cloned.1.call-start = ((), (), s32[]{:S(2)}) async-start(), calls=%async_computation.4 | async-start | bytes 1769472 | tf_op jit(solution)/shard_map/all_gather | solution.py:137
  116.7 24.5 %collective-permute-start.12 = (bf16[2,32,320]{2,1,0:T(8,128)(2,1)S(1)}, bf16[2,32,320]{2,1,0:T(8,128)(2,1)S(1)}, u32[]{:S(2)}, u32[]{:S(2)}) collective-permute-start(bf16[2,32,320]{2,1,0:T(8,128)(2,1)S(1)} %multiply_convert_fusion.1), channel_id=1, source_target_pairs={{0,48},{16,32},{32,16},{48,0},{1,49},{17,33},{33,17},{49,1},{2,50}... | collective-permute-start | bytes 122888 | tf_op jit(solution)/shard_map/ppermute | solution.py:45
  122.0 19.2 %collective-permute-start.13 = (bf16[2,32,320]{2,1,0:T(8,128)(2,1)S(1)}, bf16[2,32,320]{2,1,0:T(8,128)(2,1)S(1)}, u32[]{:S(2)}, u32[]{:S(2)}) collective-permute-start(bf16[2,32,320]{2,1,0:T(8,128)(2,1)S(1)} %multiply_convert_fusion.1), channel_id=1, source_target_pairs={{0,32},{16,48},{32,0},{48,16},{1,33},{17,49},{33,1},{49,17},{2,34}... | collective-permute-start | bytes 122888 | tf_op jit(solution)/shard_map/ppermute | solution.py:45
  123.9 17.3 %collective-permute-start.14 = (bf16[2,32,320]{2,1,0:T(8,128)(2,1)S(1)}, bf16[2,32,320]{2,1,0:T(8,128)(2,1)S(1)}, u32[]{:S(2)}, u32[]{:S(2)}) collective-permute-start(bf16[2,32,320]{2,1,0:T(8,128)(2,1)S(1)} %multiply_convert_fusion.1), channel_id=1, source_target_pairs={{0,16},{16,0},{32,48},{48,32},{1,17},{17,1},{33,49},{49,33},{2,18}... | collective-permute-start | bytes 122888 | tf_op jit(solution)/shard_map/ppermute | solution.py:45
  142.3 12.4 %collective-permute-start.7 = (bf16[2,128,432]{1,2,0:T(8,128)(2,1)S(1)}, bf16[2,128,432]{1,2,0:T(8,128)(2,1)S(1)}, u32[]{:S(2)}, u32[]{:S(2)}) collective-permute-start(bf16[2,128,432]{1,2,0:T(8,128)(2,1)S(1)} %convert_element_type.30), channel_id=1, source_target_pairs={{0,2},{2,0},{1,3},{3,1},{4,6},{6,4},{5,7},{7,5},{8,10},{10,8},{9,1... | collective-permute-start | bytes 663560 | tf_op jit(solution)/shard_map/ppermute | solution.py:36
  168.4 15.2 %collective-permute-start.15 = (bf16[4,2,128,432]{2,3,1,0:T(8,128)(2,1)S(1)}, bf16[4,2,128,432]{2,3,1,0:T(8,128)(2,1)S(1)}, u32[]{:S(2)}, u32[]{:S(2)}) collective-permute-start(bf16[4,2,128,432]{2,3,1,0:T(8,128)(2,1)S(1)} %bitcast.70), channel_id=1, source_target_pairs={{0,1},{1,0},{2,3},{3,2},{4,5},{5,4},{6,7},{7,6},{8,9},{9,8},{10,11... | collective-permute-start | bytes 2654216 | tf_op jit(solution)/shard_map/ppermute | solution.py:36
Sparse Core Ops, SparseCore 0:
  29.3 55.2 all-gather.3
  142.2 39.6 all-gather.5

commit v3 on v2

--- a/solution.py
+++ b/solution.py
@@ -141,14 +141,14 @@
     part = part.transpose(0, 2, 1).reshape(2, 8, 2 * half, -1).astype(F32).sum(1)
     rot = part + swap(part.astype(BF16), "zh").astype(F32)
     sq = lax.all_gather((rot * rot).astype(BF16), "x", axis=0)
-    mine, there = (v.reshape(-1, v.shape[-1]) for v in (sq, swap(sq, "core")))
+    mine, there = (v.reshape(8, 2 * half, -1) for v in (sq, swap(sq, "core")))
     tokens = sq_act.shape[0] // 2
     core = lax.axis_index("core")
     total = sum(
         lax.dot_general(
             g,
-            lax.dynamic_slice_in_dim(sq_act, at * tokens, tokens, 0),
-            (((0,), (0,)), ((), ())),
+            lax.dynamic_slice_in_dim(sq_act, at * tokens, tokens, 0).reshape(8, 2 * half, cols),
+            (((0, 1), (0, 1)), ((), ())),
             preferred_element_type=F32,
         )
         for g, at in ((mine, core), (there, 1 - core))

time: 195 us -> 194 us (level)
  matrix products: 5.43 us -> 3.16 us
    dot_general x2, matrix products: 4.21 us -> 1.95 us  [on_device(): lax.dot_general(g, lax.dynamic_slice_in_dim(sq_act, at * tokens, tokens,...]
where the time goes in v3:
time: 194 us; the launch traced here: 193 us
  starting transfers between devices  75.4 us (39%)
  waiting for transfers between devices  48.7 us (25%)
  blocking collectives  24.9 us (13%)
  between operations  13.8 us (7%)
  local copies, waits for them, and re-layouts  12.3 us (6%)
  other arithmetic  8.16 us (4%)
  Pallas kernels  6.61 us (3%)
  matrix products  3.16 us (2%)
    ppermute x7, starting transfers between devices, swap(): return lax.ppermute(value, axis, [(0, 1), (1, 0)])  32 us
    ppermute x9, starting transfers between devices, spread(): lax.ppermute(value, axis, [(i, i ^ k) for i in range(4)])  31.3 us
    ppermute x9, waiting for transfers between devices, spread(): lax.ppermute(value, axis, [(i, i ^ k) for i in range(4)])  19.2 us
    ppermute x7, waiting for transfers between devices, swap(): return lax.ppermute(value, axis, [(0, 1), (1, 0)])  14.5 us
    all_gather x1, blocking collectives, on_device(): sq = lax.all_gather((rot * rot).astype(BF16), 'x', axis=0)  13.6 us
    all_gather x1, waiting for transfers between devices, on_device(): sq_act = lax.all_gather(sq, 'y', axis=0, tiled=True)  11.6 us
    all_to_all x1, blocking collectives, on_device(): act = lax.all_to_all(acts.reshape(4, quarter, feats), ('zq', 'zp'), 0, 0)  11.3 us
    all_to_all x1, starting transfers between devices, on_device(): rot = lax.all_to_all(rot, 'y', 0, 0)  7.1 us
  transfers between devices with their start and end apart: 20, of which 10 were waited for; matrix products, arithmetic and copies ran while one was open for 8% of the time, Pallas kernels for 3%

profile of v3, /device:TPU:2, one launch (start us, length us, event | category | flops | bytes accessed | tf_op | source)
XLA Modules:
  0.0 193.1 jit_solution(15750890135269944624)
XLA Ops:
  6.5 1.7 copy.61.refs_2_
  8.2 6.1 %collective-permute-start = (bf16[64,1728]{1,0:T(8,128)(2,1)}, bf16[64,1728]{1,0:T(8,128)(2,1)S(1)}, u32[]{:S(2)}, u32[]{:S(2)}) collective-permute-start(bf16[64,1728]{1,0:T(8,128)(2,1)} %param.4), channel_id=1, source_target_pairs={{0,32},{32,0},{1,33},{33,1},{2,34},{34,2},{3,35},{35,3},{4,36},{36... | collective-permute-start | bytes 663560 | tf_op jit(solution)/shard_map/ppermute | solution.py:36
  14.3 0.9 copy.31
  15.2 11.3 %all_to_all.15.refs_1_ = bf16[4,32,160]{2,1,0:T(8,128)(2,1)} all-to-all(bf16[4,32,160]{2,1,0:T(8,128)(2,1)S(1)} %bitcast.89), channel_id=1, replica_groups=mesh['y'=8,'zq'=2,'zp'=2,'x'=4,'zh'=2,'core'=2] {'zq','zp'}, dimensions={0} | all-to-all | bytes 81920 | tf_op jit(solution)/shard_map/all_to_all | solution.py:113
  26.5 0.7 copy-done.4
  27.2 1.9 pad_maximum_fusion.2
  29.1 9.4 %collective-permute-start.1 = (bf16[4,32,160]{2,1,0:T(8,128)(2,1)}, bf16[4,32,160]{2,1,0:T(8,128)(2,1)S(1)}, u32[]{:S(2)}, u32[]{:S(2)}) collective-permute-start(bf16[4,32,160]{2,1,0:T(8,128)(2,1)} %get-tuple-element.13), channel_id=1, source_target_pairs={{0,2},{2,0},{1,3},{3,1},{4,6},{6,4},{5,7},{7,5},{8,10},{10,8},{9,1... | collective-permute-start | bytes 122888 | tf_op jit(solution)/shard_map/ppermute | solution.py:36
  38.5 1.0 slice.34.refs_0_
  39.5 1.5 collective-permute-done.1
  41.8 1.6 copy.32
  43.4 2.2 %collective-permute-start.2 = (bf16[256,1728]{0,1:T(8,128)(2,1)S(1)}, bf16[256,1728]{0,1:T(8,128)(2,1)S(1)}, u32[]{:S(2)}, u32[]{:S(2)}) collective-permute-start(bf16[256,1728]{0,1:T(8,128)(2,1)S(1)} %copy.32), channel_id=1, source_target_pairs={{0,16},{16,0},{1,17},{17,1},{2,18},{18,2},{3,19},{19,3},{4,20},{20... | collective-permute-start | bytes 2654216 | tf_op jit(solution)/shard_map/ppermute | solution.py:36
  45.6 3.4 %collective-permute-start.3 = (bf16[2,4,32,160]{3,2,1,0:T(8,128)(2,1)S(1)}, bf16[2,4,32,160]{3,2,1,0:T(8,128)(2,1)}, u32[]{:S(2)}, u32[]{:S(2)}) collective-permute-start(bf16[2,4,32,160]{3,2,1,0:T(8,128)(2,1)S(1)} %copy-done.3), channel_id=1, source_target_pairs={{0,12},{4,8},{8,4},{12,0},{1,13},{5,9},{9,5},{13,1},{2,14},{6,10},... | collective-permute-start | bytes 245768 | tf_op jit(solution)/shard_map/ppermute | solution.py:45
  49.0 3.0 %collective-permute-start.4 = (bf16[2,4,32,160]{3,2,1,0:T(8,128)(2,1)S(1)}, bf16[2,4,32,160]{3,2,1,0:T(8,128)(2,1)}, u32[]{:S(2)}, u32[]{:S(2)}) collective-permute-start(bf16[2,4,32,160]{3,2,1,0:T(8,128)(2,1)S(1)} %copy-done.3), channel_id=1, source_target_pairs={{0,8},{4,12},{8,0},{12,4},{1,9},{5,13},{9,1},{13,5},{2,10},{6,14},... | collective-permute-start | bytes 245768 | tf_op jit(solution)/shard_map/ppermute | solution.py:45
  52.0 3.4 %collective-permute-start.5 = (bf16[2,4,32,160]{3,2,1,0:T(8,128)(2,1)S(1)}, bf16[2,4,32,160]{3,2,1,0:T(8,128)(2,1)}, u32[]{:S(2)}, u32[]{:S(2)}) collective-permute-start(bf16[2,4,32,160]{3,2,1,0:T(8,128)(2,1)S(1)} %copy-done.3), channel_id=1, source_target_pairs={{0,4},{4,0},{8,12},{12,8},{1,5},{5,1},{9,13},{13,9},{2,6},{6,2},{1... | collective-permute-start | bytes 245768 | tf_op jit(solution)/shard_map/ppermute | solution.py:45
  55.4 0.9 slice.35.refs_0_
  56.3 2.2 %collective-permute-done.4 = bf16[2,4,32,160]{3,2,1,0:T(8,128)(2,1)} collective-permute-done((bf16[2,4,32,160]{3,2,1,0:T(8,128)(2,1)S(1)}, bf16[2,4,32,160]{3,2,1,0:T(8,128)(2,1)}, u32[]{:S(2)}, u32[]{:S(2)}) %collective-permute-start.4) | collective-permute-done | bytes 81952 | tf_op jit(solution)/shard_map/ppermute | solution.py:45
  59.1 1.1 select_bitcast_fusion.5
  60.2 0.9 pad_maximum_fusion.1.refs_1_
  61.1 3.7 %collective-permute-done.2 = bf16[256,1728]{0,1:T(8,128)(2,1)S(1)} collective-permute-done((bf16[256,1728]{0,1:T(8,128)(2,1)S(1)}, bf16[256,1728]{0,1:T(8,128)(2,1)S(1)}, u32[]{:S(2)}, u32[]{:S(2)}) %collective-permute-start.2) | collective-permute-done | bytes 884768 | tf_op jit(solution)/shard_map/ppermute | solution.py:36
  64.8 1.4 copy.34.refs_2_.low_ref.refs_1_
  66.2 1.9 collective-permute-start.8
  68.2 5.4 %collective-permute-start.10 = (bf16[160,320]{1,0:T(8,128)(2,1)S(1)}, bf16[160,320]{1,0:T(8,128)(2,1)S(1)}, u32[]{:S(2)}, u32[]{:S(2)}) collective-permute-start(bf16[160,320]{1,0:T(8,128)(2,1)S(1)} %copy-done), channel_id=1, source_target_pairs={{0,32},{16,48},{32,0},{48,16},{1,33},{17,49},{33,1},{49,17},{2,34}... | collective-permute-start | bytes 307208 | tf_op jit(solution)/shard_map/ppermute | solution.py:45
  73.6 3.1 %collective-permute-start.9 = (bf16[160,320]{1,0:T(8,128)(2,1)S(1)}, bf16[160,320]{1,0:T(8,128)(2,1)S(1)}, u32[]{:S(2)}, u32[]{:S(2)}) collective-permute-start(bf16[160,320]{1,0:T(8,128)(2,1)S(1)} %copy-done), channel_id=1, source_target_pairs={{0,48},{16,32},{32,16},{48,0},{1,49},{17,33},{33,17},{49,1},{2,50}... | collective-permute-start | bytes 307208 | tf_op jit(solution)/shard_map/ppermute | solution.py:45
  76.7 2.5 %collective-permute-start.11 = (bf16[160,320]{1,0:T(8,128)(2,1)S(1)}, bf16[160,320]{1,0:T(8,128)(2,1)S(1)}, u32[]{:S(2)}, u32[]{:S(2)}) collective-permute-start(bf16[160,320]{1,0:T(8,128)(2,1)S(1)} %copy-done), channel_id=1, source_target_pairs={{0,16},{16,0},{32,48},{48,32},{1,17},{17,1},{33,49},{49,33},{2,18}... | collective-permute-start | bytes 307208 | tf_op jit(solution)/shard_map/ppermute | solution.py:45
  79.2 3.4 %collective-permute-start.6 = (bf16[176,1728]{1,0:T(8,128)(2,1)}, bf16[176,1728]{1,0:T(8,128)(2,1)S(1)}, u32[]{:S(2)}, u32[]{:S(2)}) collective-permute-start(bf16[176,1728]{1,0:T(8,128)(2,1)} %get-tuple-element.16), channel_id=1, source_target_pairs={{0,16},{16,0},{1,17},{17,1},{2,18},{18,2},{3,19},{19,3},{4,20},{20... | collective-permute-start | bytes 1824776 | tf_op jit(solution)/shard_map/ppermute | solution.py:36
  82.6 1.1 select_bitcast_fusion.1
  84.0 1.6 collective-permute-done.11
  87.1 0.8 copy.51
  87.9 7.1 %all-to-all-start.2 = ((bf16[8,2,32,320]{3,2,1,0:T(8,128)(2,1)}), bf16[8,2,32,320]{3,2,1,0:T(8,128)(2,1)S(1)}, u32[]{:S(2)}, u32[]{:S(2)}) async-start(bf16[8,2,32,320]{3,2,1,0:T(8,128)(2,1)} %bitcast.73), calls=%async_computation.2 | async-start | bytes 786432 | tf_op jit(solution)/shard_map/all_to_all | solution.py:129
  95.0 4.1 %collective-permute-done.6.high_ref.refs_2_ = bf16[176,1728]{1,0:T(8,128)(2,1)S(1)} collective-permute-done((bf16[176,1728]{1,0:T(8,128)(2,1)}, bf16[176,1728]{1,0:T(8,128)(2,1)S(1)}, u32[]{:S(2)}, u32[]{:S(2)}) %collective-permute-start.6) | collective-permute-done | bytes 608288 | tf_op jit(solution)/shard_map/ppermute | solution.py:36
  99.1 0.8 copy-done.5
  99.9 6.6 %shard_map.49 = bf16[16,432,128]{2,1,0:T(8,128)(2,1)} custom-call(s32[1]{0:T(128)} %bitcast.zp_ref, bf16[1024,1728]{1,0:T(8,128)(2,1)} %all-gather.4.cloned.1.call-done.all_ref, bf16[432,1728]{1,0:T(8,128)(2,1)} %bitcast.79, bf16[256,1728]{1,0:T(8,128)(2,1)} %copy.34.refs_2_.low_ref.refs_1_, bf16[176,1728]{1,0:T(8,128)(2,1)} %copy-done.5), custom_call_target="tpu_custom_call" | custom-call | flops 3057647616 | bytes 3538944 | tf_op jit(solution)/shard_map/pallas_call | solution.py:88
  106.5 3.3 %all-to-all-done.2.refs_0_ = bf16[8,2,32,320]{3,2,1,0:T(8,128)(2,1)S(1)} async-done(((bf16[8,2,32,320]{3,2,1,0:T(8,128)(2,1)}), bf16[8,2,32,320]{3,2,1,0:T(8,128)(2,1)S(1)}, u32[]{:S(2)}, u32[]{:S(2)}) %all-to-all-start.2) | async-done | bytes 327712 | tf_op jit(solution)/shard_map/all_to_all | solution.py:129
  109.8 0.7 copy-done.1
  110.6 5.0 %all-to-all-start.1 = ((bf16[16,432,128]{2,1,0:T(8,128)(2,1)}), bf16[16,432,128]{2,1,0:T(8,128)(2,1)S(1)}, u32[]{:S(2)}, u32[]{:S(2)}) async-start(bf16[16,432,128]{2,1,0:T(8,128)(2,1)} %shard_map.49), calls=%async_computation.1 | async-start | bytes 3538944 | tf_op jit(solution)/shard_map/all_to_all | solution.py:140
  115.6 1.1 convert_reduce_fusion
  116.7 6.1 %collective-permute-start.12 = (bf16[2,32,320]{2,1,0:T(8,128)(2,1)S(1)}, bf16[2,32,320]{2,1,0:T(8,128)(2,1)S(1)}, u32[]{:S(2)}, u32[]{:S(2)}) collective-permute-start(bf16[2,32,320]{2,1,0:T(8,128)(2,1)S(1)} %multiply_convert_fusion.1), channel_id=1, source_target_pairs={{0,48},{16,32},{32,16},{48,0},{1,49},{17,33},{33,17},{49,1},{2,50}... | collective-permute-start | bytes 122888 | tf_op jit(solution)/shard_map/ppermute | solution.py:45
  122.8 1.9 collective-permute-start.13
  124.7 2.5 %collective-permute-start.14 = (bf16[2,32,320]{2,1,0:T(8,128)(2,1)S(1)}, bf16[2,32,320]{2,1,0:T(8,128)(2,1)S(1)}, u32[]{:S(2)}, u32[]{:S(2)}) collective-permute-start(bf16[2,32,320]{2,1,0:T(8,128)(2,1)S(1)} %multiply_convert_fusion.1), channel_id=1, source_target_pairs={{0,16},{16,0},{32,48},{48,32},{1,17},{17,1},{33,49},{49,33},{2,18}... | collective-permute-start | bytes 122888 | tf_op jit(solution)/shard_map/ppermute | solution.py:45
  127.2 14.8 %collective-permute-done.12 = bf16[2,32,320]{2,1,0:T(8,128)(2,1)S(1)} collective-permute-done((bf16[2,32,320]{2,1,0:T(8,128)(2,1)S(1)}, bf16[2,32,320]{2,1,0:T(8,128)(2,1)S(1)}, u32[]{:S(2)}, u32[]{:S(2)}) %collective-permute-start.12) | collective-permute-done | bytes 40992 | tf_op jit(solution)/shard_map/ppermute | solution.py:45
  142.1 0.7 pad_maximum_fusion.4
  143.1 7.2 %collective-permute-start.7 = (bf16[2,128,432]{1,2,0:T(8,128)(2,1)S(1)}, bf16[2,128,432]{1,2,0:T(8,128)(2,1)S(1)}, u32[]{:S(2)}, u32[]{:S(2)}) collective-permute-start(bf16[2,128,432]{1,2,0:T(8,128)(2,1)S(1)} %convert_element_type.30), channel_id=1, source_target_pairs={{0,2},{2,0},{1,3},{3,1},{4,6},{6,4},{5,7},{7,5},{8,10},{10,8},{9,1... | collective-permute-start | bytes 663560 | tf_op jit(solution)/shard_map/ppermute | solution.py:36
  150.3 5.2 %collective-permute-done.7 = bf16[2,128,432]{1,2,0:T(8,128)(2,1)S(1)} collective-permute-done((bf16[2,128,432]{1,2,0:T(8,128)(2,1)S(1)}, bf16[2,128,432]{1,2,0:T(8,128)(2,1)S(1)}, u32[]{:S(2)}, u32[]{:S(2)}) %collective-permute-start.7) | collective-permute-done | bytes 221216 | tf_op jit(solution)/shard_map/ppermute | solution.py:36
  155.6 13.6 %all-gather = bf16[8,128,432]{1,2,0:T(8,128)(2,1)S(1)} all-gather(bf16[2,128,432]{1,2,0:T(8,128)(2,1)S(1)} %multiply_convert_fusion), channel_id=2, replica_groups=mesh['y'=8,'zq'=2,'zp'=2,'x'=4,'zh'=2,'core'=2] {'x'}, dimensions={0}, use_global_device_ids=true | all-gather | bytes 1105920 | tf_op jit(solution)/shard_map/all_gather | solution.py:143
  169.2 1.9 collective-permute-start.15
  171.1 11.6 %all-gather.6.cloned.1.call-done = bf16[2048,320]{1,0:T(8,128)(2,1)} async-done(((bf16[256,320]{1,0:T(8,128)(2,1)}), bf16[2048,320]{1,0:T(8,128)(2,1)}) %all-gather.6.cloned.1.call-update) | async-done | bytes 1310736 | tf_op jit(solution)/shard_map/all_gather | solution.py:137
  182.7 1.5 constant_dynamic-slice_fusion
  184.8 1.4 fusion.3
  (47 shorter events, 4.1 us)
Async XLA Ops:
  6.5 32.0 %copy-start.2 = (bf16[1728,432]{0,1:T(8,128)(2,1)S(1)}, bf16[1728,432]{0,1:T(8,128)(2,1)}, u32[]{:S(2)}) copy-start(bf16[1728,432]{0,1:T(8,128)(2,1)} %param.6) | copy-start | bytes 4478980
  6.5 92.5 %all-gather.4.cloned.1.call-start = ((), (), s32[]{:S(2)}) async-start(), calls=%async_computation.3 | async-start | bytes 4128768 | tf_op jit(solution)/shard_map/all_gather | solution.py:115
  8.2 18.3 %collective-permute-start = (bf16[64,1728]{1,0:T(8,128)(2,1)}, bf16[64,1728]{1,0:T(8,128)(2,1)S(1)}, u32[]{:S(2)}, u32[]{:S(2)}) collective-permute-start(bf16[64,1728]{1,0:T(8,128)(2,1)} %param.4), channel_id=1, source_target_pairs={{0,32},{32,0},{1,33},{33,1},{2,34},{34,2},{3,35},{35,3},{4,36},{36... | collective-permute-start | bytes 663560 | tf_op jit(solution)/shard_map/ppermute | solution.py:36
  26.5 0.7 copy-start.4
  27.2 13.8 %copy-start.6 = (bf16[4,32,160]{2,1,0:T(8,128)(2,1)S(1)}, bf16[4,32,160]{2,1,0:T(8,128)(2,1)}, u32[]{:S(2)}) copy-start(bf16[4,32,160]{2,1,0:T(8,128)(2,1)} %get-tuple-element.13) | copy-start | bytes 122884
  29.1 11.9 %collective-permute-start.1 = (bf16[4,32,160]{2,1,0:T(8,128)(2,1)}, bf16[4,32,160]{2,1,0:T(8,128)(2,1)S(1)}, u32[]{:S(2)}, u32[]{:S(2)}) collective-permute-start(bf16[4,32,160]{2,1,0:T(8,128)(2,1)} %get-tuple-element.13), channel_id=1, source_target_pairs={{0,2},{2,0},{1,3},{3,1},{4,6},{6,4},{5,7},{7,5},{8,10},{10,8},{9,1... | collective-permute-start | bytes 122888 | tf_op jit(solution)/shard_map/ppermute | solution.py:36
  41.8 3.8 %copy-start.3 = (bf16[2,4,32,160]{3,2,1,0:T(8,128)(2,1)S(1)}, bf16[2,4,32,160]{3,2,1,0:T(8,128)(2,1)}, u32[]{:S(2)}) copy-start(bf16[2,4,32,160]{3,2,1,0:T(8,128)(2,1)} %get-tuple-element.15) | copy-start | bytes 245764
  43.4 21.5 %collective-permute-start.2 = (bf16[256,1728]{0,1:T(8,128)(2,1)S(1)}, bf16[256,1728]{0,1:T(8,128)(2,1)S(1)}, u32[]{:S(2)}, u32[]{:S(2)}) collective-permute-start(bf16[256,1728]{0,1:T(8,128)(2,1)S(1)} %copy.32), channel_id=1, source_target_pairs={{0,16},{16,0},{1,17},{17,1},{2,18},{18,2},{3,19},{19,3},{4,20},{20... | collective-permute-start | bytes 2654216 | tf_op jit(solution)/shard_map/ppermute | solution.py:36
  45.6 10.7 %collective-permute-start.3 = (bf16[2,4,32,160]{3,2,1,0:T(8,128)(2,1)S(1)}, bf16[2,4,32,160]{3,2,1,0:T(8,128)(2,1)}, u32[]{:S(2)}, u32[]{:S(2)}) collective-permute-start(bf16[2,4,32,160]{3,2,1,0:T(8,128)(2,1)S(1)} %copy-done.3), channel_id=1, source_target_pairs={{0,12},{4,8},{8,4},{12,0},{1,13},{5,9},{9,5},{13,1},{2,14},{6,10},... | collective-permute-start | bytes 245768 | tf_op jit(solution)/shard_map/ppermute | solution.py:45
  49.0 9.5 %collective-permute-start.4 = (bf16[2,4,32,160]{3,2,1,0:T(8,128)(2,1)S(1)}, bf16[2,4,32,160]{3,2,1,0:T(8,128)(2,1)}, u32[]{:S(2)}, u32[]{:S(2)}) collective-permute-start(bf16[2,4,32,160]{3,2,1,0:T(8,128)(2,1)S(1)} %copy-done.3), channel_id=1, source_target_pairs={{0,8},{4,12},{8,0},{12,4},{1,9},{5,13},{9,1},{13,5},{2,10},{6,14},... | collective-permute-start | bytes 245768 | tf_op jit(solution)/shard_map/ppermute | solution.py:45
  52.0 7.1 %collective-permute-start.5 = (bf16[2,4,32,160]{3,2,1,0:T(8,128)(2,1)S(1)}, bf16[2,4,32,160]{3,2,1,0:T(8,128)(2,1)}, u32[]{:S(2)}, u32[]{:S(2)}) collective-permute-start(bf16[2,4,32,160]{3,2,1,0:T(8,128)(2,1)S(1)} %copy-done.3), channel_id=1, source_target_pairs={{0,4},{4,0},{8,12},{12,8},{1,5},{5,1},{9,13},{13,9},{2,6},{6,2},{1... | collective-permute-start | bytes 245768 | tf_op jit(solution)/shard_map/ppermute | solution.py:45
  61.1 7.0 %copy-start = (bf16[160,320]{1,0:T(8,128)(2,1)S(1)}, bf16[160,320]{1,0:T(8,128)(2,1)}, u32[]{:S(2)}) copy-start(bf16[160,320]{1,0:T(8,128)(2,1)} %get-tuple-element.18) | copy-start | bytes 307204
  66.2 16.3 %collective-permute-start.8 = (bf16[4,2,4,32,160]{4,3,2,1,0:T(8,128)(2,1)}, bf16[4,2,4,32,160]{4,3,2,1,0:T(8,128)(2,1)S(1)}, u32[]{:S(2)}, u32[]{:S(2)}) collective-permute-start(bf16[4,2,4,32,160]{4,3,2,1,0:T(8,128)(2,1)} %get-tuple-element.17), channel_id=1, source_target_pairs={{0,1},{1,0},{2,3},{3,2},{4,5},{5,4},{6,7},{7,6},{8,9},{9,8},{10,11... | collective-permute-start | bytes 983048 | tf_op jit(solution)/shard_map/ppermute | solution.py:36
  68.2 15.8 %collective-permute-start.10 = (bf16[160,320]{1,0:T(8,128)(2,1)S(1)}, bf16[160,320]{1,0:T(8,128)(2,1)S(1)}, u32[]{:S(2)}, u32[]{:S(2)}) collective-permute-start(bf16[160,320]{1,0:T(8,128)(2,1)S(1)} %copy-done), channel_id=1, source_target_pairs={{0,32},{16,48},{32,0},{48,16},{1,33},{17,49},{33,1},{49,17},{2,34}... | collective-permute-start | bytes 307208 | tf_op jit(solution)/shard_map/ppermute | solution.py:45
  73.6 10.4 %collective-permute-start.9 = (bf16[160,320]{1,0:T(8,128)(2,1)S(1)}, bf16[160,320]{1,0:T(8,128)(2,1)S(1)}, u32[]{:S(2)}, u32[]{:S(2)}) collective-permute-start(bf16[160,320]{1,0:T(8,128)(2,1)S(1)} %copy-done), channel_id=1, source_target_pairs={{0,48},{16,32},{32,16},{48,0},{1,49},{17,33},{33,17},{49,1},{2,50}... | collective-permute-start | bytes 307208 | tf_op jit(solution)/shard_map/ppermute | solution.py:45
  76.7 8.9 %collective-permute-start.11 = (bf16[160,320]{1,0:T(8,128)(2,1)S(1)}, bf16[160,320]{1,0:T(8,128)(2,1)S(1)}, u32[]{:S(2)}, u32[]{:S(2)}) collective-permute-start(bf16[160,320]{1,0:T(8,128)(2,1)S(1)} %copy-done), channel_id=1, source_target_pairs={{0,16},{16,0},{32,48},{48,32},{1,17},{17,1},{33,49},{49,33},{2,18}... | collective-permute-start | bytes 307208 | tf_op jit(solution)/shard_map/ppermute | solution.py:45
  79.2 19.9 %collective-permute-start.6 = (bf16[176,1728]{1,0:T(8,128)(2,1)}, bf16[176,1728]{1,0:T(8,128)(2,1)S(1)}, u32[]{:S(2)}, u32[]{:S(2)}) collective-permute-start(bf16[176,1728]{1,0:T(8,128)(2,1)} %get-tuple-element.16), channel_id=1, source_target_pairs={{0,16},{16,0},{1,17},{17,1},{2,18},{18,2},{3,19},{19,3},{4,20},{20... | collective-permute-start | bytes 1824776 | tf_op jit(solution)/shard_map/ppermute | solution.py:36
  87.9 21.9 %all-to-all-start.2 = ((bf16[8,2,32,320]{3,2,1,0:T(8,128)(2,1)}), bf16[8,2,32,320]{3,2,1,0:T(8,128)(2,1)S(1)}, u32[]{:S(2)}, u32[]{:S(2)}) async-start(bf16[8,2,32,320]{3,2,1,0:T(8,128)(2,1)} %bitcast.73), calls=%async_computation.2 | async-start | bytes 786432 | tf_op jit(solution)/shard_map/all_to_all | solution.py:129
  99.1 0.8 copy-start.5
  109.8 0.7 copy-start.1
  110.6 32.3 %all-to-all-start.1 = ((bf16[16,432,128]{2,1,0:T(8,128)(2,1)}), bf16[16,432,128]{2,1,0:T(8,128)(2,1)S(1)}, u32[]{:S(2)}, u32[]{:S(2)}) async-start(bf16[16,432,128]{2,1,0:T(8,128)(2,1)} %shard_map.49), calls=%async_computation.1 | async-start | bytes 3538944 | tf_op jit(solution)/shard_map/all_to_all | solution.py:140
  115.6 67.2 %all-gather.6.cloned.1.call-start = ((), (), s32[]{:S(2)}) async-start(), calls=%async_computation.4 | async-start | bytes 1769472 | tf_op jit(solution)/shard_map/all_gather | solution.py:137
  116.7 25.3 %collective-permute-start.12 = (bf16[2,32,320]{2,1,0:T(8,128)(2,1)S(1)}, bf16[2,32,320]{2,1,0:T(8,128)(2,1)S(1)}, u32[]{:S(2)}, u32[]{:S(2)}) collective-permute-start(bf16[2,32,320]{2,1,0:T(8,128)(2,1)S(1)} %multiply_convert_fusion.1), channel_id=1, source_target_pairs={{0,48},{16,32},{32,16},{48,0},{1,49},{17,33},{33,17},{49,1},{2,50}... | collective-permute-start | bytes 122888 | tf_op jit(solution)/shard_map/ppermute | solution.py:45
  122.8 19.2 %collective-permute-start.13 = (bf16[2,32,320]{2,1,0:T(8,128)(2,1)S(1)}, bf16[2,32,320]{2,1,0:T(8,128)(2,1)S(1)}, u32[]{:S(2)}, u32[]{:S(2)}) collective-permute-start(bf16[2,32,320]{2,1,0:T(8,128)(2,1)S(1)} %multiply_convert_fusion.1), channel_id=1, source_target_pairs={{0,32},{16,48},{32,0},{48,16},{1,33},{17,49},{33,1},{49,17},{2,34}... | collective-permute-start | bytes 122888 | tf_op jit(solution)/shard_map/ppermute | solution.py:45
  124.7 17.3 %collective-permute-start.14 = (bf16[2,32,320]{2,1,0:T(8,128)(2,1)S(1)}, bf16[2,32,320]{2,1,0:T(8,128)(2,1)S(1)}, u32[]{:S(2)}, u32[]{:S(2)}) collective-permute-start(bf16[2,32,320]{2,1,0:T(8,128)(2,1)S(1)} %multiply_convert_fusion.1), channel_id=1, source_target_pairs={{0,16},{16,0},{32,48},{48,32},{1,17},{17,1},{33,49},{49,33},{2,18}... | collective-permute-start | bytes 122888 | tf_op jit(solution)/shard_map/ppermute | solution.py:45
  143.1 12.4 %collective-permute-start.7 = (bf16[2,128,432]{1,2,0:T(8,128)(2,1)S(1)}, bf16[2,128,432]{1,2,0:T(8,128)(2,1)S(1)}, u32[]{:S(2)}, u32[]{:S(2)}) collective-permute-start(bf16[2,128,432]{1,2,0:T(8,128)(2,1)S(1)} %convert_element_type.30), channel_id=1, source_target_pairs={{0,2},{2,0},{1,3},{3,1},{4,6},{6,4},{5,7},{7,5},{8,10},{10,8},{9,1... | collective-permute-start | bytes 663560 | tf_op jit(solution)/shard_map/ppermute | solution.py:36
  169.2 15.6 %collective-permute-start.15 = (bf16[4,2,128,432]{2,3,1,0:T(8,128)(2,1)S(1)}, bf16[4,2,128,432]{2,3,1,0:T(8,128)(2,1)S(1)}, u32[]{:S(2)}, u32[]{:S(2)}) collective-permute-start(bf16[4,2,128,432]{2,3,1,0:T(8,128)(2,1)S(1)} %bitcast.75), channel_id=1, source_target_pairs={{0,1},{1,0},{2,3},{3,2},{4,5},{5,4},{6,7},{7,6},{8,9},{9,8},{10,11... | collective-permute-start | bytes 2654216 | tf_op jit(solution)/shard_map/ppermute | solution.py:36
Sparse Core Ops, SparseCore 0:
  29.3 55.2 all-gather.3
  143.0 39.7 all-gather.5

commit v4 on v3

--- a/solution.py
+++ b/solution.py
@@ -120,7 +120,7 @@
     other_basis = [swap(send, "zp")]
     basis = spread(act_basis, ("zq", "zp"))
     act = spread(act, "x")
-    send, act = tie([own_basis[cut:], act], other_basis)
+    send, act, basis = tie([own_basis[cut:], act, basis], other_basis)
     other_basis.append(swap(send, "zp"))
     act = ordered("core", act, swap(act, "core"))
     act = act.reshape(16, 4, quarter, feats)

time: 194 us -> 193 us (level)
  waiting for transfers between devices: 48.7 us -> 46.6 us
    ppermute x7, waiting for transfers between devices: 14.5 us -> 10.3 us  [swap(): return lax.ppermute(value, axis, [(0, 1), (1, 0)])]
    unnamed x16 -> x18, local copies, waits for them, and re-layouts: 4.82 us -> 5.55 us
  transfers between devices with their start and end apart: 20 -> 20, of which waited for: 10 -> 8; matrix products, arithmetic and copies ran while one was open for 8% -> 9% of each run, Pallas kernels for 3% -> 3%
where the time goes in v4:
time: 193 us; the launch traced here: 192 us
  starting transfers between devices  74.8 us (39%)
  waiting for transfers between devices  46.6 us (24%)
  blocking collectives  24.9 us (13%)
  local copies, waits for them, and re-layouts  13.9 us (7%)
  between operations  13.8 us (7%)
  other arithmetic  8.13 us (4%)
  Pallas kernels  6.61 us (3%)
  matrix products  3.14 us (2%)
    ppermute x7, starting transfers between devices, swap(): return lax.ppermute(value, axis, [(0, 1), (1, 0)])  32.4 us
    ppermute x9, starting transfers between devices, spread(): lax.ppermute(value, axis, [(i, i ^ k) for i in range(4)])  30.4 us
    ppermute x9, waiting for transfers between devices, spread(): lax.ppermute(value, axis, [(i, i ^ k) for i in range(4)])  20.2 us
    all_gather x1, blocking collectives, on_device(): sq = lax.all_gather((rot * rot).astype(BF16), 'x', axis=0)  13.6 us
    all_gather x1, waiting for transfers between devices, on_device(): sq_act = lax.all_gather(sq, 'y', axis=0, tiled=True)  12 us
    all_to_all x1, blocking collectives, on_device(): act = lax.all_to_all(acts.reshape(4, quarter, feats), ('zq', 'zp'), 0, 0)  11.3 us
    ppermute x7, waiting for transfers between devices, swap(): return lax.ppermute(value, axis, [(0, 1), (1, 0)])  10.3 us
    all_to_all x1, starting transfers between devices, on_device(): rot = lax.all_to_all(rot, 'y', 0, 0)  7.1 us
  transfers between devices with their start and end apart: 20, of which 8 were waited for; matrix products, arithmetic and copies ran while one was open for 9% of the time, Pallas kernels for 3%

profile of v4, /device:TPU:2, one launch (start us, length us, event | category | flops | bytes accessed | tf_op | source)
XLA Modules:
  0.0 191.8 jit_solution(8385732085204283706)
XLA Ops:
  6.5 1.7 copy.63.refs_2_
  8.2 6.1 %collective-permute-start = (bf16[64,1728]{1,0:T(8,128)(2,1)}, bf16[64,1728]{1,0:T(8,128)(2,1)S(1)}, u32[]{:S(2)}, u32[]{:S(2)}) collective-permute-start(bf16[64,1728]{1,0:T(8,128)(2,1)} %param.4), channel_id=1, source_target_pairs={{0,32},{32,0},{1,33},{33,1},{2,34},{34,2},{3,35},{35,3},{4,36},{36... | collective-permute-start | bytes 663560 | tf_op jit(solution)/shard_map/ppermute | solution.py:36
  14.3 0.9 copy.32
  15.2 11.3 %all_to_all.15.refs_1_ = bf16[4,32,160]{2,1,0:T(8,128)(2,1)} all-to-all(bf16[4,32,160]{2,1,0:T(8,128)(2,1)S(1)} %bitcast.109), channel_id=1, replica_groups=mesh['y'=8,'zq'=2,'zp'=2,'x'=4,'zh'=2,'core'=2] {'zq','zp'}, dimensions={0} | all-to-all | bytes 81920 | tf_op jit(solution)/shard_map/all_to_all | solution.py:113
  26.5 0.7 copy-done.5
  27.2 1.9 pad_maximum_fusion.3
  29.1 9.4 %collective-permute-start.1 = (bf16[4,32,160]{2,1,0:T(8,128)(2,1)}, bf16[4,32,160]{2,1,0:T(8,128)(2,1)S(1)}, u32[]{:S(2)}, u32[]{:S(2)}) collective-permute-start(bf16[4,32,160]{2,1,0:T(8,128)(2,1)} %get-tuple-element.14), channel_id=1, source_target_pairs={{0,2},{2,0},{1,3},{3,1},{4,6},{6,4},{5,7},{7,5},{8,10},{10,8},{9,1... | collective-permute-start | bytes 122888 | tf_op jit(solution)/shard_map/ppermute | solution.py:36
  38.5 1.0 slice.50.refs_0_
  39.6 1.5 collective-permute-done.1
  41.1 0.7 pad_maximum_fusion.6.refs_1_
  41.8 1.6 copy.33
  43.4 2.2 %collective-permute-start.2 = (bf16[256,1728]{0,1:T(8,128)(2,1)S(1)}, bf16[256,1728]{0,1:T(8,128)(2,1)}, u32[]{:S(2)}, u32[]{:S(2)}) collective-permute-start(bf16[256,1728]{0,1:T(8,128)(2,1)S(1)} %copy.33), channel_id=1, source_target_pairs={{0,16},{16,0},{1,17},{17,1},{2,18},{18,2},{3,19},{19,3},{4,20},{20... | collective-permute-start | bytes 2654216 | tf_op jit(solution)/shard_map/ppermute | solution.py:36
  45.6 3.4 %collective-permute-start.3 = (bf16[2,4,32,160]{3,2,1,0:T(8,128)(2,1)S(1)}, bf16[2,4,32,160]{3,2,1,0:T(8,128)(2,1)S(1)}, u32[]{:S(2)}, u32[]{:S(2)}) collective-permute-start(bf16[2,4,32,160]{3,2,1,0:T(8,128)(2,1)S(1)} %copy-done.3), channel_id=1, source_target_pairs={{0,12},{4,8},{8,4},{12,0},{1,13},{5,9},{9,5},{13,1},{2,14},{6,10},... | collective-permute-start | bytes 245768 | tf_op jit(solution)/shard_map/ppermute | solution.py:45
  49.0 3.0 %collective-permute-start.4 = (bf16[2,4,32,160]{3,2,1,0:T(8,128)(2,1)S(1)}, bf16[2,4,32,160]{3,2,1,0:T(8,128)(2,1)S(1)}, u32[]{:S(2)}, u32[]{:S(2)}) collective-permute-start(bf16[2,4,32,160]{3,2,1,0:T(8,128)(2,1)S(1)} %copy-done.3), channel_id=1, source_target_pairs={{0,8},{4,12},{8,0},{12,4},{1,9},{5,13},{9,1},{13,5},{2,10},{6,14},... | collective-permute-start | bytes 245768 | tf_op jit(solution)/shard_map/ppermute | solution.py:45
  52.0 3.4 %collective-permute-start.5 = (bf16[2,4,32,160]{3,2,1,0:T(8,128)(2,1)S(1)}, bf16[2,4,32,160]{3,2,1,0:T(8,128)(2,1)S(1)}, u32[]{:S(2)}, u32[]{:S(2)}) collective-permute-start(bf16[2,4,32,160]{3,2,1,0:T(8,128)(2,1)S(1)} %copy-done.3), channel_id=1, source_target_pairs={{0,4},{4,0},{8,12},{12,8},{1,5},{5,1},{9,13},{13,9},{2,6},{6,2},{1... | collective-permute-start | bytes 245768 | tf_op jit(solution)/shard_map/ppermute | solution.py:45
  55.4 0.9 slice.51.refs_0_
  56.3 5.9 %collective-permute-start.6 = (bf16[160,320]{1,0:T(8,128)(2,1)S(1)}, bf16[160,320]{1,0:T(8,128)(2,1)S(1)}, u32[]{:S(2)}, u32[]{:S(2)}) collective-permute-start(bf16[160,320]{1,0:T(8,128)(2,1)S(1)} %copy-done.4), channel_id=1, source_target_pairs={{0,48},{16,32},{32,16},{48,0},{1,49},{17,33},{33,17},{49,1},{2,50}... | collective-permute-start | bytes 307208 | tf_op jit(solution)/shard_map/ppermute | solution.py:45
  62.2 1.9 %collective-permute-start.7 = (bf16[160,320]{1,0:T(8,128)(2,1)S(1)}, bf16[160,320]{1,0:T(8,128)(2,1)S(1)}, u32[]{:S(2)}, u32[]{:S(2)}) collective-permute-start(bf16[160,320]{1,0:T(8,128)(2,1)S(1)} %copy-done.4), channel_id=1, source_target_pairs={{0,32},{16,48},{32,0},{48,16},{1,33},{17,49},{33,1},{49,17},{2,34}... | collective-permute-start | bytes 307208 | tf_op jit(solution)/shard_map/ppermute | solution.py:45
  64.1 2.5 %collective-permute-start.8 = (bf16[160,320]{1,0:T(8,128)(2,1)S(1)}, bf16[160,320]{1,0:T(8,128)(2,1)S(1)}, u32[]{:S(2)}, u32[]{:S(2)}) collective-permute-start(bf16[160,320]{1,0:T(8,128)(2,1)S(1)} %copy-done.4), channel_id=1, source_target_pairs={{0,16},{16,0},{32,48},{48,32},{1,17},{17,1},{33,49},{49,33},{2,18}... | collective-permute-start | bytes 307208 | tf_op jit(solution)/shard_map/ppermute | solution.py:45
  66.7 0.9 pad_maximum_fusion.1.refs_1_
  67.6 5.1 %collective-permute-done.6 = bf16[160,320]{1,0:T(8,128)(2,1)S(1)} collective-permute-done((bf16[160,320]{1,0:T(8,128)(2,1)S(1)}, bf16[160,320]{1,0:T(8,128)(2,1)S(1)}, u32[]{:S(2)}, u32[]{:S(2)}) %collective-permute-start.6) | collective-permute-done | bytes 102432 | tf_op jit(solution)/shard_map/ppermute | solution.py:45
  73.1 0.9 pad_maximum_fusion.2.refs_2_
  74.0 2.2 %copy.35.refs_3_.low_ref.refs_1_ = bf16[256,1728]{1,0:T(8,128)(2,1)} copy(bf16[256,1728]{0,1:T(8,128)(2,1)} %collective-permute-done.2) | data formatting | bytes 1769472 | tf_op jit(solution)/shard_map/ppermute | solution.py:36
  76.3 1.9 collective-permute-start.11
  78.2 3.8 %collective-permute-start.9 = (bf16[176,1728]{1,0:T(8,128)(2,1)}, bf16[176,1728]{1,0:T(8,128)(2,1)S(1)}, u32[]{:S(2)}, u32[]{:S(2)}) collective-permute-start(bf16[176,1728]{1,0:T(8,128)(2,1)} %get-tuple-element.18), channel_id=1, source_target_pairs={{0,16},{16,0},{1,17},{17,1},{2,18},{18,2},{3,19},{19,3},{4,20},{20... | collective-permute-start | bytes 1824776 | tf_op jit(solution)/shard_map/ppermute | solution.py:36
  82.0 1.1 select_bitcast_fusion.1
  83.4 0.7 copy-done
  85.6 0.8 copy.52
  86.4 7.1 %all-to-all-start.2 = ((bf16[8,2,32,320]{3,2,1,0:T(8,128)(2,1)}), bf16[8,2,32,320]{3,2,1,0:T(8,128)(2,1)S(1)}, u32[]{:S(2)}, u32[]{:S(2)}) async-start(bf16[8,2,32,320]{3,2,1,0:T(8,128)(2,1)} %bitcast.93), calls=%async_computation.2 | async-start | bytes 786432 | tf_op jit(solution)/shard_map/all_to_all | solution.py:129
  93.5 3.6 %collective-permute-done.9.high_ref.refs_2_ = bf16[176,1728]{1,0:T(8,128)(2,1)S(1)} collective-permute-done((bf16[176,1728]{1,0:T(8,128)(2,1)}, bf16[176,1728]{1,0:T(8,128)(2,1)S(1)}, u32[]{:S(2)}, u32[]{:S(2)}) %collective-permute-start.9) | collective-permute-done | bytes 608288 | tf_op jit(solution)/shard_map/ppermute | solution.py:36
  97.0 0.8 copy-done.6
  97.9 6.6 %shard_map.49 = bf16[16,432,128]{2,1,0:T(8,128)(2,1)} custom-call(s32[1]{0:T(128)} %bitcast.zp_ref, bf16[1024,1728]{1,0:T(8,128)(2,1)} %all-gather.4.cloned.1.call-done.all_ref, bf16[432,1728]{1,0:T(8,128)(2,1)} %bitcast.99, bf16[256,1728]{1,0:T(8,128)(2,1)} %copy.35.refs_3_.low_ref.refs_1_, bf16[176,1728]{1,0:T(8,128)(2,1)} %copy-done.6), custom_call_target="tpu_custom_call" | custom-call | flops 3057647616 | bytes 3538944 | tf_op jit(solution)/shard_map/pallas_call | solution.py:88
  104.5 4.0 %all-to-all-done.2.refs_0_ = bf16[8,2,32,320]{3,2,1,0:T(8,128)(2,1)S(1)} async-done(((bf16[8,2,32,320]{3,2,1,0:T(8,128)(2,1)}), bf16[8,2,32,320]{3,2,1,0:T(8,128)(2,1)S(1)}, u32[]{:S(2)}, u32[]{:S(2)}) %all-to-all-start.2) | async-done | bytes 327712 | tf_op jit(solution)/shard_map/all_to_all | solution.py:129
  108.5 0.8 copy-done.1
  109.3 4.9 %all-to-all-start.1 = ((bf16[16,432,128]{2,1,0:T(8,128)(2,1)}), bf16[16,432,128]{2,1,0:T(8,128)(2,1)S(1)}, u32[]{:S(2)}, u32[]{:S(2)}) async-start(bf16[16,432,128]{2,1,0:T(8,128)(2,1)} %shard_map.49), calls=%async_computation.1 | async-start | bytes 3538944 | tf_op jit(solution)/shard_map/all_to_all | solution.py:140
  114.2 1.1 convert_reduce_fusion
  115.3 5.9 %collective-permute-start.12 = (bf16[2,32,320]{2,1,0:T(8,128)(2,1)S(1)}, bf16[2,32,320]{2,1,0:T(8,128)(2,1)S(1)}, u32[]{:S(2)}, u32[]{:S(2)}) collective-permute-start(bf16[2,32,320]{2,1,0:T(8,128)(2,1)S(1)} %multiply_convert_fusion.1), channel_id=1, source_target_pairs={{0,48},{16,32},{32,16},{48,0},{1,49},{17,33},{33,17},{49,1},{2,50}... | collective-permute-start | bytes 122888 | tf_op jit(solution)/shard_map/ppermute | solution.py:45
  121.2 1.9 %collective-permute-start.13 = (bf16[2,32,320]{2,1,0:T(8,128)(2,1)S(1)}, bf16[2,32,320]{2,1,0:T(8,128)(2,1)S(1)}, u32[]{:S(2)}, u32[]{:S(2)}) collective-permute-start(bf16[2,32,320]{2,1,0:T(8,128)(2,1)S(1)} %multiply_convert_fusion.1), channel_id=1, source_target_pairs={{0,32},{16,48},{32,0},{48,16},{1,33},{17,49},{33,1},{49,17},{2,34}... | collective-permute-start | bytes 122888 | tf_op jit(solution)/shard_map/ppermute | solution.py:45
  123.1 2.5 %collective-permute-start.14 = (bf16[2,32,320]{2,1,0:T(8,128)(2,1)S(1)}, bf16[2,32,320]{2,1,0:T(8,128)(2,1)S(1)}, u32[]{:S(2)}, u32[]{:S(2)}) collective-permute-start(bf16[2,32,320]{2,1,0:T(8,128)(2,1)S(1)} %multiply_convert_fusion.1), channel_id=1, source_target_pairs={{0,16},{16,0},{32,48},{48,32},{1,17},{17,1},{33,49},{49,33},{2,18}... | collective-permute-start | bytes 122888 | tf_op jit(solution)/shard_map/ppermute | solution.py:45
  125.6 14.8 %collective-permute-done.12 = bf16[2,32,320]{2,1,0:T(8,128)(2,1)S(1)} collective-permute-done((bf16[2,32,320]{2,1,0:T(8,128)(2,1)S(1)}, bf16[2,32,320]{2,1,0:T(8,128)(2,1)S(1)}, u32[]{:S(2)}, u32[]{:S(2)}) %collective-permute-start.12) | collective-permute-done | bytes 40992 | tf_op jit(solution)/shard_map/ppermute | solution.py:45
  140.5 0.7 pad_maximum_fusion.5
  141.5 7.2 %collective-permute-start.10 = (bf16[2,128,432]{1,2,0:T(8,128)(2,1)S(1)}, bf16[2,128,432]{1,2,0:T(8,128)(2,1)S(1)}, u32[]{:S(2)}, u32[]{:S(2)}) collective-permute-start(bf16[2,128,432]{1,2,0:T(8,128)(2,1)S(1)} %convert_element_type.30), channel_id=1, source_target_pairs={{0,2},{2,0},{1,3},{3,1},{4,6},{6,4},{5,7},{7,5},{8,10},{10,8},{9,1... | collective-permute-start | bytes 663560 | tf_op jit(solution)/shard_map/ppermute | solution.py:36
  148.7 5.2 %collective-permute-done.10 = bf16[2,128,432]{1,2,0:T(8,128)(2,1)S(1)} collective-permute-done((bf16[2,128,432]{1,2,0:T(8,128)(2,1)S(1)}, bf16[2,128,432]{1,2,0:T(8,128)(2,1)S(1)}, u32[]{:S(2)}, u32[]{:S(2)}) %collective-permute-start.10) | collective-permute-done | bytes 221216 | tf_op jit(solution)/shard_map/ppermute | solution.py:36
  154.0 13.6 %all-gather = bf16[8,128,432]{1,2,0:T(8,128)(2,1)S(1)} all-gather(bf16[2,128,432]{1,2,0:T(8,128)(2,1)S(1)} %multiply_convert_fusion), channel_id=2, replica_groups=mesh['y'=8,'zq'=2,'zp'=2,'x'=4,'zh'=2,'core'=2] {'x'}, dimensions={0}, use_global_device_ids=true | all-gather | bytes 1105920 | tf_op jit(solution)/shard_map/all_gather | solution.py:143
  167.6 1.9 collective-permute-start.15
  169.5 12.0 %all-gather.6.cloned.1.call-done = bf16[2048,320]{1,0:T(8,128)(2,1)} async-done(((bf16[256,320]{1,0:T(8,128)(2,1)}), bf16[2048,320]{1,0:T(8,128)(2,1)}) %all-gather.6.cloned.1.call-update) | async-done | bytes 1310736 | tf_op jit(solution)/shard_map/all_gather | solution.py:137
  181.5 1.5 constant_dynamic-slice_fusion
  183.6 1.4 fusion.1
  (51 shorter events, 3.3 us)
Async XLA Ops:
  6.5 32.0 %copy-start.2 = (bf16[1728,432]{0,1:T(8,128)(2,1)S(1)}, bf16[1728,432]{0,1:T(8,128)(2,1)}, u32[]{:S(2)}) copy-start(bf16[1728,432]{0,1:T(8,128)(2,1)} %param.6) | copy-start | bytes 4478980
  6.5 90.5 %all-gather.4.cloned.1.call-start = ((), (), s32[]{:S(2)}) async-start(), calls=%async_computation.3 | async-start | bytes 4128768 | tf_op jit(solution)/shard_map/all_gather | solution.py:115
  8.2 18.3 %collective-permute-start = (bf16[64,1728]{1,0:T(8,128)(2,1)}, bf16[64,1728]{1,0:T(8,128)(2,1)S(1)}, u32[]{:S(2)}, u32[]{:S(2)}) collective-permute-start(bf16[64,1728]{1,0:T(8,128)(2,1)} %param.4), channel_id=1, source_target_pairs={{0,32},{32,0},{1,33},{33,1},{2,34},{34,2},{3,35},{35,3},{4,36},{36... | collective-permute-start | bytes 663560 | tf_op jit(solution)/shard_map/ppermute | solution.py:36
  26.5 0.7 copy-start.5
  27.2 13.8 %copy-start.7 = (bf16[4,32,160]{2,1,0:T(8,128)(2,1)S(1)}, bf16[4,32,160]{2,1,0:T(8,128)(2,1)}, u32[]{:S(2)}) copy-start(bf16[4,32,160]{2,1,0:T(8,128)(2,1)} %get-tuple-element.14) | copy-start | bytes 122884
  29.1 11.9 %collective-permute-start.1 = (bf16[4,32,160]{2,1,0:T(8,128)(2,1)}, bf16[4,32,160]{2,1,0:T(8,128)(2,1)S(1)}, u32[]{:S(2)}, u32[]{:S(2)}) collective-permute-start(bf16[4,32,160]{2,1,0:T(8,128)(2,1)} %get-tuple-element.14), channel_id=1, source_target_pairs={{0,2},{2,0},{1,3},{3,1},{4,6},{6,4},{5,7},{7,5},{8,10},{10,8},{9,1... | collective-permute-start | bytes 122888 | tf_op jit(solution)/shard_map/ppermute | solution.py:36
  41.8 3.8 %copy-start.3 = (bf16[2,4,32,160]{3,2,1,0:T(8,128)(2,1)S(1)}, bf16[2,4,32,160]{3,2,1,0:T(8,128)(2,1)}, u32[]{:S(2)}) copy-start(bf16[2,4,32,160]{3,2,1,0:T(8,128)(2,1)} %get-tuple-element.16) | copy-start | bytes 245764
  41.8 14.5 %copy-start.4 = (bf16[160,320]{1,0:T(8,128)(2,1)S(1)}, bf16[160,320]{1,0:T(8,128)(2,1)}, u32[]{:S(2)}) copy-start(bf16[160,320]{1,0:T(8,128)(2,1)} %get-tuple-element.17) | copy-start | bytes 307204
  43.4 30.7 %collective-permute-start.2 = (bf16[256,1728]{0,1:T(8,128)(2,1)S(1)}, bf16[256,1728]{0,1:T(8,128)(2,1)}, u32[]{:S(2)}, u32[]{:S(2)}) collective-permute-start(bf16[256,1728]{0,1:T(8,128)(2,1)S(1)} %copy.33), channel_id=1, source_target_pairs={{0,16},{16,0},{1,17},{17,1},{2,18},{18,2},{3,19},{19,3},{4,20},{20... | collective-permute-start | bytes 2654216 | tf_op jit(solution)/shard_map/ppermute | solution.py:36
  45.6 16.6 %collective-permute-start.3 = (bf16[2,4,32,160]{3,2,1,0:T(8,128)(2,1)S(1)}, bf16[2,4,32,160]{3,2,1,0:T(8,128)(2,1)S(1)}, u32[]{:S(2)}, u32[]{:S(2)}) collective-permute-start(bf16[2,4,32,160]{3,2,1,0:T(8,128)(2,1)S(1)} %copy-done.3), channel_id=1, source_target_pairs={{0,12},{4,8},{8,4},{12,0},{1,13},{5,9},{9,5},{13,1},{2,14},{6,10},... | collective-permute-start | bytes 245768 | tf_op jit(solution)/shard_map/ppermute | solution.py:45
  49.0 15.2 %collective-permute-start.4 = (bf16[2,4,32,160]{3,2,1,0:T(8,128)(2,1)S(1)}, bf16[2,4,32,160]{3,2,1,0:T(8,128)(2,1)S(1)}, u32[]{:S(2)}, u32[]{:S(2)}) collective-permute-start(bf16[2,4,32,160]{3,2,1,0:T(8,128)(2,1)S(1)} %copy-done.3), channel_id=1, source_target_pairs={{0,8},{4,12},{8,0},{12,4},{1,9},{5,13},{9,1},{13,5},{2,10},{6,14},... | collective-permute-start | bytes 245768 | tf_op jit(solution)/shard_map/ppermute | solution.py:45
  52.0 14.6 %collective-permute-start.5 = (bf16[2,4,32,160]{3,2,1,0:T(8,128)(2,1)S(1)}, bf16[2,4,32,160]{3,2,1,0:T(8,128)(2,1)S(1)}, u32[]{:S(2)}, u32[]{:S(2)}) collective-permute-start(bf16[2,4,32,160]{3,2,1,0:T(8,128)(2,1)S(1)} %copy-done.3), channel_id=1, source_target_pairs={{0,4},{4,0},{8,12},{12,8},{1,5},{5,1},{9,13},{13,9},{2,6},{6,2},{1... | collective-permute-start | bytes 245768 | tf_op jit(solution)/shard_map/ppermute | solution.py:45
  56.3 16.5 %collective-permute-start.6 = (bf16[160,320]{1,0:T(8,128)(2,1)S(1)}, bf16[160,320]{1,0:T(8,128)(2,1)S(1)}, u32[]{:S(2)}, u32[]{:S(2)}) collective-permute-start(bf16[160,320]{1,0:T(8,128)(2,1)S(1)} %copy-done.4), channel_id=1, source_target_pairs={{0,48},{16,32},{32,16},{48,0},{1,49},{17,33},{33,17},{49,1},{2,50}... | collective-permute-start | bytes 307208 | tf_op jit(solution)/shard_map/ppermute | solution.py:45
  62.2 10.5 %collective-permute-start.7 = (bf16[160,320]{1,0:T(8,128)(2,1)S(1)}, bf16[160,320]{1,0:T(8,128)(2,1)S(1)}, u32[]{:S(2)}, u32[]{:S(2)}) collective-permute-start(bf16[160,320]{1,0:T(8,128)(2,1)S(1)} %copy-done.4), channel_id=1, source_target_pairs={{0,32},{16,48},{32,0},{48,16},{1,33},{17,49},{33,1},{49,17},{2,34}... | collective-permute-start | bytes 307208 | tf_op jit(solution)/shard_map/ppermute | solution.py:45
  64.1 8.9 %collective-permute-start.8 = (bf16[160,320]{1,0:T(8,128)(2,1)S(1)}, bf16[160,320]{1,0:T(8,128)(2,1)S(1)}, u32[]{:S(2)}, u32[]{:S(2)}) collective-permute-start(bf16[160,320]{1,0:T(8,128)(2,1)S(1)} %copy-done.4), channel_id=1, source_target_pairs={{0,16},{16,0},{32,48},{48,32},{1,17},{17,1},{33,49},{49,33},{2,18}... | collective-permute-start | bytes 307208 | tf_op jit(solution)/shard_map/ppermute | solution.py:45
  76.3 5.7 %collective-permute-start.11 = (bf16[4,2,4,32,160]{4,3,2,1,0:T(8,128)(2,1)}, bf16[4,2,4,32,160]{4,3,2,1,0:T(8,128)(2,1)S(1)}, u32[]{:S(2)}, u32[]{:S(2)}) collective-permute-start(bf16[4,2,4,32,160]{4,3,2,1,0:T(8,128)(2,1)} %get-tuple-element.19), channel_id=1, source_target_pairs={{0,1},{1,0},{2,3},{3,2},{4,5},{5,4},{6,7},{7,6},{8,9},{9,8},{10,11... | collective-permute-start | bytes 983048 | tf_op jit(solution)/shard_map/ppermute | solution.py:36
  78.2 18.9 %collective-permute-start.9 = (bf16[176,1728]{1,0:T(8,128)(2,1)}, bf16[176,1728]{1,0:T(8,128)(2,1)S(1)}, u32[]{:S(2)}, u32[]{:S(2)}) collective-permute-start(bf16[176,1728]{1,0:T(8,128)(2,1)} %get-tuple-element.18), channel_id=1, source_target_pairs={{0,16},{16,0},{1,17},{17,1},{2,18},{18,2},{3,19},{19,3},{4,20},{20... | collective-permute-start | bytes 1824776 | tf_op jit(solution)/shard_map/ppermute | solution.py:36
  83.1 1.0 copy-start
  86.4 22.2 %all-to-all-start.2 = ((bf16[8,2,32,320]{3,2,1,0:T(8,128)(2,1)}), bf16[8,2,32,320]{3,2,1,0:T(8,128)(2,1)S(1)}, u32[]{:S(2)}, u32[]{:S(2)}) async-start(bf16[8,2,32,320]{3,2,1,0:T(8,128)(2,1)} %bitcast.93), calls=%async_computation.2 | async-start | bytes 786432 | tf_op jit(solution)/shard_map/all_to_all | solution.py:129
  97.0 0.8 copy-start.6
  108.5 0.8 copy-start.1
  109.3 31.9 %all-to-all-start.1 = ((bf16[16,432,128]{2,1,0:T(8,128)(2,1)}), bf16[16,432,128]{2,1,0:T(8,128)(2,1)S(1)}, u32[]{:S(2)}, u32[]{:S(2)}) async-start(bf16[16,432,128]{2,1,0:T(8,128)(2,1)} %shard_map.49), calls=%async_computation.1 | async-start | bytes 3538944 | tf_op jit(solution)/shard_map/all_to_all | solution.py:140
  114.1 67.3 %all-gather.6.cloned.1.call-start = ((), (), s32[]{:S(2)}) async-start(), calls=%async_computation.4 | async-start | bytes 1769472 | tf_op jit(solution)/shard_map/all_gather | solution.py:137
  115.3 25.0 %collective-permute-start.12 = (bf16[2,32,320]{2,1,0:T(8,128)(2,1)S(1)}, bf16[2,32,320]{2,1,0:T(8,128)(2,1)S(1)}, u32[]{:S(2)}, u32[]{:S(2)}) collective-permute-start(bf16[2,32,320]{2,1,0:T(8,128)(2,1)S(1)} %multiply_convert_fusion.1), channel_id=1, source_target_pairs={{0,48},{16,32},{32,16},{48,0},{1,49},{17,33},{33,17},{49,1},{2,50}... | collective-permute-start | bytes 122888 | tf_op jit(solution)/shard_map/ppermute | solution.py:45
  121.2 19.2 %collective-permute-start.13 = (bf16[2,32,320]{2,1,0:T(8,128)(2,1)S(1)}, bf16[2,32,320]{2,1,0:T(8,128)(2,1)S(1)}, u32[]{:S(2)}, u32[]{:S(2)}) collective-permute-start(bf16[2,32,320]{2,1,0:T(8,128)(2,1)S(1)} %multiply_convert_fusion.1), channel_id=1, source_target_pairs={{0,32},{16,48},{32,0},{48,16},{1,33},{17,49},{33,1},{49,17},{2,34}... | collective-permute-start | bytes 122888 | tf_op jit(solution)/shard_map/ppermute | solution.py:45
  123.1 17.3 %collective-permute-start.14 = (bf16[2,32,320]{2,1,0:T(8,128)(2,1)S(1)}, bf16[2,32,320]{2,1,0:T(8,128)(2,1)S(1)}, u32[]{:S(2)}, u32[]{:S(2)}) collective-permute-start(bf16[2,32,320]{2,1,0:T(8,128)(2,1)S(1)} %multiply_convert_fusion.1), channel_id=1, source_target_pairs={{0,16},{16,0},{32,48},{48,32},{1,17},{17,1},{33,49},{49,33},{2,18}... | collective-permute-start | bytes 122888 | tf_op jit(solution)/shard_map/ppermute | solution.py:45
  141.5 12.4 %collective-permute-start.10 = (bf16[2,128,432]{1,2,0:T(8,128)(2,1)S(1)}, bf16[2,128,432]{1,2,0:T(8,128)(2,1)S(1)}, u32[]{:S(2)}, u32[]{:S(2)}) collective-permute-start(bf16[2,128,432]{1,2,0:T(8,128)(2,1)S(1)} %convert_element_type.30), channel_id=1, source_target_pairs={{0,2},{2,0},{1,3},{3,1},{4,6},{6,4},{5,7},{7,5},{8,10},{10,8},{9,1... | collective-permute-start | bytes 663560 | tf_op jit(solution)/shard_map/ppermute | solution.py:36
  167.6 16.0 %collective-permute-start.15 = (bf16[4,2,128,432]{2,3,1,0:T(8,128)(2,1)S(1)}, bf16[4,2,128,432]{2,3,1,0:T(8,128)(2,1)S(1)}, u32[]{:S(2)}, u32[]{:S(2)}) collective-permute-start(bf16[4,2,128,432]{2,3,1,0:T(8,128)(2,1)S(1)} %bitcast.95), channel_id=1, source_target_pairs={{0,1},{1,0},{2,3},{3,2},{4,5},{5,4},{6,7},{7,6},{8,9},{9,8},{10,11... | collective-permute-start | bytes 2654216 | tf_op jit(solution)/shard_map/ppermute | solution.py:36
Sparse Core Ops, SparseCore 0:
  29.3 55.2 all-gather.3
  141.3 40.1 all-gather.5
